TPU v7x, 32 devices: a whole 2x2x4 slice. The times are simulated.
32 devices in a mesh: grp: 4 (over x, core), inner: 8 (over z, y).
Axes of the slice: x: 2, y: 2, z: 4, core: 2. Of those that a mesh axis runs over, the one named last changes fastest.
Arguments:
- moe_input: bfloat16 [4096, 2048], P(('grp', 'inner')), may hold values from -6 to 6
- out_grad: bfloat16 [4096, 2048], P(('grp', 'inner')), may hold values from -1.5 to 1.5
- context: bfloat16 [4096, 4096], P('grp', 'inner'), may hold values from -0.119628906 to 0.119628906
- gate_scale: float32 [32, 256], P(('grp', 'inner')), may hold values from 0.2 to 1
- selected: int32 [32, 256], replicated, may hold values from 0 to 4095, as said below
- w_gate: bfloat16 [32, 2048, 768], P(('grp', 'inner')), may hold values from -0.125 to 0.125
- w_up: bfloat16 [32, 2048, 768], P(('grp', 'inner')), may hold values from -0.125 to 0.125
- w_down: bfloat16 [32, 768, 2048], P(('grp', 'inner')), may hold values from -0.21875 to 0.21875
- w_out: bfloat16 [4096, 2048], P('inner'), may hold values from -0.09375 to 0.09375
Outputs:
- grad_gate: bfloat16 [32, 2048, 768], P(('grp', 'inner'))
- grad_up: bfloat16 [32, 2048, 768], P(('grp', 'inner'))
- grad_down: bfloat16 [32, 768, 2048], P(('grp', 'inner'))
- grad_context: bfloat16 [4096, 4096], P('grp', 'inner')
- grad_out: bfloat16 [4096, 2048], P('inner', 'grp')
Inputs may be any that keep to these rules, and one draw needn't show every extreme that they name: `selected`: each expert's 256 token indices are distinct; at most 16 of them lie among the 128 tokens of one device (tokens d * 128 to (d + 1) * 128 - 1), and every expert takes exactly 16 from some device.
All inputs are finite; a program needn't handle non-finite values.
Results may differ from a plain program's by a relative error of at most 0.014.
Values may be sent and summed in bfloat16 or wider, within the bound.
A program may use at most 128 MiB of HBM per device.

v0:
```python
import jax
import jax.numpy as jnp
from jax import lax
from jax.sharding import PartitionSpec as P


def expert_backward(rows_in, rows_grad, scales, gate_w, up_w, down_w):
    gate_pre = jnp.dot(rows_in, gate_w, preferred_element_type=jnp.float32)
    up_pre = jnp.dot(rows_in, up_w, preferred_element_type=jnp.float32)
    sig = jax.nn.sigmoid(gate_pre)
    silu = gate_pre * sig
    hidden = (silu * up_pre).astype(jnp.bfloat16)
    scaled = (rows_grad.astype(jnp.float32) * scales[:, None]).astype(jnp.bfloat16)
    outer = (((0,), (0,)), ((), ()))
    inner_dims = (((1,), (1,)), ((), ()))
    grad_down = lax.dot_general(hidden, scaled, outer, preferred_element_type=jnp.float32).astype(
        jnp.bfloat16
    )
    back_hidden = lax.dot_general(scaled, down_w, inner_dims, preferred_element_type=jnp.float32)
    back_gate = (back_hidden * up_pre * sig * (1.0 + gate_pre * (1.0 - sig))).astype(jnp.bfloat16)
    back_up = (back_hidden * silu).astype(jnp.bfloat16)
    grad_gate = lax.dot_general(
        rows_in, back_gate, outer, preferred_element_type=jnp.float32
    ).astype(jnp.bfloat16)
    grad_up = lax.dot_general(rows_in, back_up, outer, preferred_element_type=jnp.float32).astype(
        jnp.bfloat16
    )
    row_grad = lax.dot_general(back_gate, gate_w, inner_dims, preferred_element_type=jnp.float32)
    row_grad = row_grad + lax.dot_general(
        back_up, up_w, inner_dims, preferred_element_type=jnp.float32
    )
    return (grad_gate, grad_up, grad_down, row_grad.astype(jnp.bfloat16))


def body(moe_input, out_grad, context, gate_scale, selected, w_gate, w_up, w_down, w_out):
    groups = lax.axis_size("grp")
    inner_count = lax.axis_size("inner")
    devices = groups * inner_count
    tok_rows = moe_input.shape[0]
    width = moe_input.shape[1]
    capacity = selected.shape[1]
    most = max(4, (2 * capacity + devices - 1) // devices)
    device = lax.axis_index("grp") * inner_count + lax.axis_index("inner")
    owner = selected // tok_rows
    mine = owner == device
    ordinal = jnp.cumsum(mine.astype(jnp.int32), axis=1) - 1
    slot_ids = jnp.arange(most, dtype=jnp.int32)
    match_slot = mine[:, :, None] & (ordinal[:, :, None] == slot_ids[None, None, :])
    local_token = selected - device * tok_rows
    token_table = jnp.sum(jnp.where(match_slot, local_token[:, :, None], 0), axis=1)
    filled = jnp.any(match_slot, axis=1)
    token_ids = jnp.arange(tok_rows, dtype=jnp.int32)
    picker = (
        (token_table.reshape(-1)[:, None] == token_ids[None, :]) & filled.reshape(-1)[:, None]
    ).astype(jnp.bfloat16)
    send_input = (
        jnp.dot(picker, moe_input, preferred_element_type=jnp.float32)
        .astype(jnp.bfloat16)
        .reshape(devices, most, width)
    )
    send_grad = (
        jnp.dot(picker, out_grad, preferred_element_type=jnp.float32)
        .astype(jnp.bfloat16)
        .reshape(devices, most, width)
    )
    my_owner = lax.dynamic_index_in_dim(owner, device, 0, keepdims=False)
    slot_range = jnp.arange(capacity, dtype=jnp.int32)
    same_owner = (my_owner[:, None] == my_owner[None, :]) & (
        slot_range[:, None] > slot_range[None, :]
    )
    ranking = jnp.sum(same_owner.astype(jnp.int32), axis=1)
    position = my_owner * most + ranking
    placer = (position[:, None] == jnp.arange(devices * most, dtype=jnp.int32)[None, :]).astype(
        jnp.bfloat16
    )
    recv_input, recv_grad = (
        lax.all_to_all(send_input, ("grp", "inner"), split_axis=0, concat_axis=0, tiled=True),
        lax.all_to_all(send_grad, ("grp", "inner"), split_axis=0, concat_axis=0, tiled=True),
    )
    rows_in = jnp.dot(
        placer, recv_input.reshape(-1, width), preferred_element_type=jnp.float32
    ).astype(jnp.bfloat16)
    rows_grad = jnp.dot(
        placer, recv_grad.reshape(-1, width), preferred_element_type=jnp.float32
    ).astype(jnp.bfloat16)
    grad_gate, grad_up, grad_down, row_grad = expert_backward(
        rows_in, rows_grad, gate_scale[0], w_gate[0], w_up[0], w_down[0]
    )
    placed = lax.dot_general(
        placer, row_grad, (((0,), (0,)), ((), ())), preferred_element_type=jnp.float32
    ).astype(jnp.bfloat16)
    returned = lax.all_to_all(
        placed.reshape(devices, most, width),
        ("grp", "inner"),
        split_axis=0,
        concat_axis=0,
        tiled=True,
    )
    moe_back = lax.dot_general(
        picker,
        returned.reshape(-1, width),
        (((0,), (0,)), ((), ())),
        preferred_element_type=jnp.float32,
    )
    total = (out_grad.astype(jnp.float32) + moe_back).astype(jnp.bfloat16)
    piece = lax.all_gather(total, "inner", axis=0, tiled=True)
    part_context = lax.dot_general(
        piece, w_out, (((1,), (1,)), ((), ())), preferred_element_type=jnp.float32
    )
    grad_ctx = part_context
    grad_proj = lax.dot_general(
        context, piece, (((0,), (0,)), ((), ())), preferred_element_type=jnp.float32
    )
    grad_ctx, grad_proj = (grad_ctx, grad_proj)
    proj_share = lax.psum_scatter(
        grad_proj.astype(jnp.bfloat16), "grp", scatter_dimension=1, tiled=True
    )
    return (
        grad_gate[None],
        grad_up[None],
        grad_down[None],
        grad_ctx.astype(jnp.bfloat16),
        proj_share,
    )


def solution(mesh):
    placed = (
        P(("grp", "inner"), None),
        P(("grp", "inner"), None),
        P("grp", "inner"),
        P(("grp", "inner"), None),
        P(),
        P(("grp", "inner"), None, None),
        P(("grp", "inner"), None, None),
        P(("grp", "inner"), None, None),
        P("inner", None),
    )
    return jax.shard_map(
        body,
        mesh=mesh,
        in_specs=placed,
        out_specs=(
            P(("grp", "inner"), None, None),
            P(("grp", "inner"), None, None),
            P(("grp", "inner"), None, None),
            P("grp", "inner"),
            P("inner", "grp"),
        ),
        check_vma=False,
    )
```

profile of v0, /device:TPU:0, one launch (start us, length us, event | category | flops | bytes accessed | tf_op | source)
XLA Modules:
  0.0 309.1 jit_solution(11916370909237510283)
XLA Ops:
  7.2 0.0 copy-start
  7.2 0.9 convert_bitcast_fusion
  8.1 0.8 broadcast_subtract_fusion
  8.9 0.6 reduce-window.6
  9.5 0.2 slice_reduce_fusion
  9.7 0.1 copy_bitcast_fusion
  9.8 0.6 fusion.28
  10.4 0.6 select_reduce_fusion
  11.1 0.1 eq.71
  11.1 0.1 and.32
  11.2 3.1 %convolution_convert_fusion.6 = bf16[512,2048]{1,0:T(8,128)(2,1)} fusion(bf16[128,2048]{1,0:T(8,128)(2,1)} %param.9, s32[512]{0:T(512)S(1)} %eq.71, pred[512]{0:T(512)(128)(4,1)S(1)} %and.32), kind=kOutput, calls=%fused_computation.19 | convolution fusion | flops 269615104 | bytes 2624000 | tf_op jit(solution)/shard_map/dot_general | solution.py:57
  14.4 7.4 %all-to-all-start = ((bf16[32,16,2048]{2,1,0:T(8,128)(2,1)}), bf16[32,16,2048]{2,1,0:T(8,128)(2,1)}, u32[]{:S(2)}, u32[]{:S(2)}) async-start(bf16[32,16,2048]{2,1,0:T(8,128)(2,1)} %bitcast.67), calls=%async_computation | async-start | bytes 4194304 | tf_op jit(solution)/shard_map/all_to_all | solution.py:77
  21.8 3.1 %convolution_convert_fusion.5 = bf16[512,2048]{1,0:T(8,128)(2,1)} fusion(bf16[128,2048]{1,0:T(8,128)(2,1)} %param.10, s32[512]{0:T(512)S(1)} %eq.71, pred[512]{0:T(512)(128)(4,1)S(1)} %and.32), kind=kOutput, calls=%fused_computation.18 | convolution fusion | flops 269615104 | bytes 2624000 | tf_op jit(solution)/shard_map/dot_general | solution.py:62
  24.9 46.9 %all-to-all-done = bf16[32,16,2048]{2,1,0:T(8,128)(2,1)} async-done(((bf16[32,16,2048]{2,1,0:T(8,128)(2,1)}), bf16[32,16,2048]{2,1,0:T(8,128)(2,1)}, u32[]{:S(2)}, u32[]{:S(2)}) %all-to-all-start) | async-done | bytes 2097184 | tf_op jit(solution)/shard_map/all_to_all | solution.py:77
  71.9 3.5 %all-to-all-start.1 = ((bf16[32,16,2048]{2,1,0:T(8,128)(2,1)}), bf16[32,16,2048]{2,1,0:T(8,128)(2,1)}, u32[]{:S(2)}, u32[]{:S(2)}) async-start(bf16[32,16,2048]{2,1,0:T(8,128)(2,1)} %bitcast.66), calls=%async_computation.1 | async-start | bytes 4194304 | tf_op jit(solution)/shard_map/all_to_all | solution.py:78
  75.3 0.0 all-gather.2.cloned.1.call-start
  75.4 0.0 copy-start.1
  75.4 0.2 convert_reduce_fusion
  75.6 2.5 convolution_convert_fusion.8
  78.1 0.0 copy-done.1
  78.1 0.0 copy-start.4
  78.1 1.9 fusion.2
  80.0 0.0 copy-done.4
  80.0 0.0 copy-done
  80.0 0.0 copy-start.9
  80.0 1.9 fusion.6
  82.0 43.4 %all-to-all-done.1 = bf16[32,16,2048]{2,1,0:T(8,128)(2,1)} async-done(((bf16[32,16,2048]{2,1,0:T(8,128)(2,1)}), bf16[32,16,2048]{2,1,0:T(8,128)(2,1)}, u32[]{:S(2)}, u32[]{:S(2)}) %all-to-all-start.1) | async-done | bytes 2097184 | tf_op jit(solution)/shard_map/all_to_all | solution.py:78
  125.4 0.0 copy-start.7
  125.4 0.0 copy-done.9
  125.4 2.5 fusion.22
  127.9 0.0 copy-done.7
  127.9 0.0 copy-start.10
  127.9 0.0 copy-start.2
  128.0 3.8 %multiply_convert_fusion.1 = (bf16[256,768]{1,0:T(8,128)(2,1)}, bf16[256,768]{1,0:T(8,128)(2,1)S(1)}) fusion(f32[256,768]{1,0:T(8,128)} %fusion.2, f32[256,768]{1,0:T(8,128)} %fusion.6, bf16[256,2048]{1,0:T(8,128)(2,1)S(1)} %fusion.22, bf16[1,768,2048]{2,1,0:T(8,128)(2,1)S(1)} %copy-done.7), kind=kOutput, calls=%fused_computation.32 | convolution fusion | flops 807862272 | bytes 6553600 | tf_op jit(solution)/shard_map/dot_general | solution.py:19
  131.7 0.0 copy-done.10
  131.7 0.0 copy-done.2
  131.7 2.4 fusion
  134.1 4.6 %convolution_convert_fusion.4 = bf16[512,2048]{1,0:T(8,128)(2,1)} fusion(f32[256,2048]{1,0:T(8,128)} %fusion, bf16[256,768]{1,0:T(8,128)(2,1)} %get-tuple-element.23, bf16[1,2048,768]{2,1,0:T(8,128)(2,1)S(1)} %copy-done, s32[256]{0:T(256)S(1)} %multiply_add_fusion), kind=kOutput, calls=%fused_computation.14 | convolution fusion | flops 1344405504 | bytes 7734272 | tf_op jit(solution)/shard_map/dot_general | solution.py:89
  138.7 0.0 copy-start.3
  138.7 52.9 %all_to_all.15 = bf16[32,16,2048]{2,1,0:T(8,128)(2,1)S(1)} all-to-all(bf16[32,16,2048]{2,1,0:T(8,128)(2,1)} %bitcast.69), channel_id=1, replica_groups=mesh['grp'=4,'inner'=8] {'grp','inner'}, dimensions={0} | all-to-all | bytes 4194304 | tf_op jit(solution)/shard_map/all_to_all | solution.py:92
  191.6 0.0 copy-done.3
  191.6 1.4 fusion.23
  193.0 0.0 all-gather.2.cloned.1.call-update
  193.0 0.2 reduce-scatter.2.cloned.1.call-start
  193.3 70.9 %all-gather.2.cloned.1.call-done = bf16[1024,2048]{1,0:T(8,128)(2,1)} async-done(((bf16[128,2048]{1,0:T(8,128)(2,1)}), bf16[1024,2048]{1,0:T(8,128)(2,1)}) %all-gather.2.cloned.1.call-update) | async-done | bytes 4194320 | tf_op jit(solution)/shard_map/all_gather | solution.py:106
  264.2 6.2 %fusion.16 = bf16[512,2048]{0,1:T(8,128)(2,1)} fusion(bf16[1024,2048]{1,0:T(8,128)(2,1)} %all-gather.2.cloned.1.call-done, bf16[1024,512]{1,0:T(8,128)(2,1)} %param.11), kind=kOutput, calls=%fused_computation.21 | convolution fusion | flops 2148532224 | bytes 7340032 | tf_op jit(solution)/shard_map/dot_general | solution.py:111
  270.3 0.0 reduce-scatter.2.cloned.1.call-update
  270.4 0.0 copy-start.5
  270.4 4.1 %fusion.11 = bf16[1,2048,768]{2,1,0:T(8,128)(2,1)} fusion(bf16[256,2048]{1,0:T(8,128)(2,1)} %copy-done.4, bf16[256,768]{1,0:T(8,128)(2,1)} %get-tuple-element.23), kind=kOutput, calls=%fused_computation.16 | convolution fusion | flops 806879232 | bytes 4587520 | tf_op jit(solution)/shard_map/dot_general | solution.py:25
  274.5 0.0 copy-done.5
  274.5 0.0 copy-start.11
  274.5 0.0 copy-start.12
  274.5 0.0 copy-start.13
  274.5 2.7 fusion.10
  277.2 0.0 copy-done.11
  277.2 0.0 copy-done.12
  277.2 0.0 copy-done.13
  277.2 0.0 copy-start.8
  277.2 2.7 fusion.12
  279.9 0.3 copy-done.6
  280.3 1.1 copy-done.8
  281.3 3.3 %convolution_convert_fusion.9 = bf16[1024,512]{1,0:T(8,128)(2,1)} fusion(bf16[1024,2048]{1,0:T(8,128)(2,1)S(1)} %copy-done.6, bf16[512,2048]{1,0:T(8,128)(2,1)S(1)} %copy-done.8), kind=kOutput, calls=%fused_computation.30 | convolution fusion | flops 2148007936 | bytes 7340032 | tf_op jit(solution)/shard_map/dot_general | solution.py:107
  284.7 15.5 %reduce-scatter.2.cloned.1.call-done = bf16[512,512]{0,1:T(8,128)(2,1)} async-done(((bf16[512,2048]{0,1:T(8,128)(2,1)}), bf16[512,512]{0,1:T(8,128)(2,1)}) %reduce-scatter.2.cloned.1.call-update) | async-done | bytes 524304 | tf_op jit(solution)/shard_map/reduce_scatter | solution.py:115
  300.2 2.0 copy.21
  (6 shorter events, 0.1 us)
Async XLA Ops:
  7.2 72.9 %copy-start = (bf16[1,2048,768]{2,1,0:T(8,128)(2,1)S(1)}, bf16[1,2048,768]{2,1,0:T(8,128)(2,1)}, u32[]{:S(2)}) copy-start(bf16[1,2048,768]{2,1,0:T(8,128)(2,1)} %param.15) | copy-start | bytes 9437188
  14.4 57.5 %all-to-all-start = ((bf16[32,16,2048]{2,1,0:T(8,128)(2,1)}), bf16[32,16,2048]{2,1,0:T(8,128)(2,1)}, u32[]{:S(2)}, u32[]{:S(2)}) async-start(bf16[32,16,2048]{2,1,0:T(8,128)(2,1)} %bitcast.67), calls=%async_computation | async-start | bytes 4194304 | tf_op jit(solution)/shard_map/all_to_all | solution.py:77
  71.9 53.5 %all-to-all-start.1 = ((bf16[32,16,2048]{2,1,0:T(8,128)(2,1)}), bf16[32,16,2048]{2,1,0:T(8,128)(2,1)}, u32[]{:S(2)}, u32[]{:S(2)}) async-start(bf16[32,16,2048]{2,1,0:T(8,128)(2,1)} %bitcast.66), calls=%async_computation.1 | async-start | bytes 4194304 | tf_op jit(solution)/shard_map/all_to_all | solution.py:78
  75.3 188.8 %all-gather.2.cloned.1.call-start = ((), (), s32[]{:S(2)}) async-start(), calls=%async_computation.4 | async-start | bytes 4718592 | tf_op jit(solution)/shard_map/all_gather | solution.py:106
  75.4 2.7 copy-start.1
  78.1 1.9 copy-start.4
  80.0 45.4 %copy-start.9 = (f32[1,256]{1,0:T(1,128)S(1)}, f32[1,256]{1,0:T(1,128)}, u32[]{:S(2)}) copy-start(f32[1,256]{1,0:T(1,128)} %param.12) | copy-start | bytes 3076
  125.4 2.5 copy-start.7
  127.9 3.8 %copy-start.10 = (bf16[256,2048]{1,0:T(8,128)(2,1)}, bf16[256,2048]{1,0:T(8,128)(2,1)S(1)}, u32[]{:S(2)}) copy-start(bf16[256,2048]{1,0:T(8,128)(2,1)S(1)} %fusion.22) | copy-start | bytes 3145732
  127.9 3.8 %copy-start.2 = (bf16[1,2048,768]{2,1,0:T(8,128)(2,1)S(1)}, bf16[1,2048,768]{2,1,0:T(8,128)(2,1)}, u32[]{:S(2)}) copy-start(bf16[1,2048,768]{2,1,0:T(8,128)(2,1)} %param.14) | copy-start | bytes 9437188
  138.7 52.9 %copy-start.3 = (bf16[128,2048]{1,0:T(8,128)(2,1)S(1)}, bf16[128,2048]{1,0:T(8,128)(2,1)}, u32[]{:S(2)}) copy-start(bf16[128,2048]{1,0:T(8,128)(2,1)} %param.10) | copy-start | bytes 1572868
  193.0 107.2 %reduce-scatter.2.cloned.1.call-start = ((), (), s32[]{:S(2)}) async-start(), calls=%async_computation.5 | async-start | bytes 2621440 | tf_op jit(solution)/shard_map/reduce_scatter | solution.py:115
  270.4 4.1 %copy-start.5 = (bf16[256,2048]{1,0:T(8,128)(2,1)S(1)}, bf16[256,2048]{1,0:T(8,128)(2,1)}, u32[]{:S(2)}) copy-start(bf16[256,2048]{1,0:T(8,128)(2,1)} %copy-done.4) | copy-start | bytes 3145732
  274.5 2.7 copy-start.11
  274.5 2.7 copy-start.12
  274.5 2.7 copy-start.13
  277.2 3.1 copy-start.6
  277.2 4.1 %copy-start.8 = (bf16[512,2048]{1,0:T(8,128)(2,1)S(1)}, bf16[512,2048]{1,0:T(8,128)(2,1)}, u32[]{:S(2)}) copy-start(bf16[512,2048]{1,0:T(8,128)(2,1)} %param.17) | copy-start | bytes 6291460
Sparse Core Ops, SparseCore 0:
  193.2 70.9 all-gather.1
  270.5 29.6 reduce-scatter.1
where the time goes:
time: 310 us; the launch traced here: 309 us
  waiting for transfers between devices  177 us (57%)
  blocking collectives  52.9 us (17%)
  matrix products  46.2 us (15%)
  between operations  14.2 us (5%)
  starting transfers between devices  11.2 us (4%)
  local copies, waits for them, and re-layouts  3.87 us (1%)
  other arithmetic  3.86 us (1%)
    all_gather x1, waiting for transfers between devices, body(): piece = lax.all_gather(total, 'inner', axis=0, tiled=True)  70.9 us
    all_to_all x1, blocking collectives, body(): lax.all_to_all(placed.reshape(devices, most, width), ('grp', 'inner'), sp...  52.9 us
    all_to_all x1, waiting for transfers between devices, body(): lax.all_to_all(send_input, ('grp', 'inner'), split_axis=0, concat_axis=0,...  46.9 us
    all_to_all x1, waiting for transfers between devices, body(): lax.all_to_all(send_grad, ('grp', 'inner'), split_axis=0, concat_axis=0,...  43.4 us
    reduce_scatter x1, waiting for transfers between devices, body(): lax.psum_scatter(grad_proj.astype(jnp.bfloat16), 'grp', scatter_dimension...  15.5 us
    all_to_all x1, starting transfers between devices, body(): lax.all_to_all(send_input, ('grp', 'inner'), split_axis=0, concat_axis=0,...  7.43 us
  transfers between devices with their start and end apart: 4, of which 4 were waited for; matrix products, arithmetic and copies ran while one was open for 7% of the time, Pallas kernels for 0%

commit v1 on v0

v1 whole, which is shorter than its diff:
```python
import functools

import jax
import jax.numpy as jnp
from jax import lax
from jax.experimental import pallas as pl
from jax.experimental.pallas import tpu as pltpu
from jax.sharding import PartitionSpec as P

MESH = pl.DeviceIdType.MESH


def split_inner(inner):
    across = 1
    while (2 * across) * (2 * across) <= inner:
        across *= 2
    return inner // across, across


def place():
    groups = lax.axis_size("grp")
    inner = lax.axis_size("inner")
    nz, ny = split_inner(inner)
    g = lax.axis_index("grp")
    i = lax.axis_index("inner")
    z = i // ny
    y = i % ny
    return groups, nz, ny, g, z, y


def at_plane(k, z, ny):
    return (k // ny, z * ny + k % ny)


def greet(g, z, y, nz, ny, planes):
    me = g * ny + y
    barrier = pltpu.get_barrier_semaphore()

    @pl.when(z > 0)
    def _():
        pl.semaphore_signal(barrier, inc=1, device_id=(g, (z - 1) * ny + y), device_id_type=MESH)

    @pl.when(z < nz - 1)
    def _():
        pl.semaphore_signal(barrier, inc=1, device_id=(g, (z + 1) * ny + y), device_id_type=MESH)

    def one(k, carry):
        peer = lax.rem(me + k, planes)
        pl.semaphore_signal(barrier, inc=1, device_id=at_plane(peer, z, ny), device_id_type=MESH)
        return carry

    lax.fori_loop(1, planes, one, 0)
    beside = jnp.where(z > 0, 1, 0) + jnp.where(z < nz - 1, 1, 0)
    pl.semaphore_wait(barrier, planes - 1 + beside)


def remote(src, dst, send, recv, device):
    return pltpu.make_async_remote_copy(
        src_ref=src, dst_ref=dst, send_sem=send, recv_sem=recv, device_id=device, device_id_type=MESH
    )


def dispatch_kernel(
    chunk, x_ref, pick_ref, place_ref, out_ref, gat, stage, recv,
    up_s, up_r, down_s, down_r, plane_s, plane_r,
):
    groups, nz, ny, g, z, y = place()
    planes = groups * ny
    me = g * ny + y
    rows, width = x_ref.shape[1:]
    slots = stage.shape[1] // planes
    parts = width // chunk
    items = 2 * parts
    above = (g, (z + 1) * ny + y)
    below = (g, (z - 1) * ny + y)
    greet(g, z, y, nz, ny, planes)

    def cols(i):
        return pl.ds(pl.multiple_of((i % parts) * chunk, chunk), chunk)

    def block(i, h):
        return gat.at[i // parts, pl.ds(pl.multiple_of(h * rows, rows), rows), cols(i)]

    def up(i, h, s):
        src = x_ref.at[i // parts, :, cols(i)] if s == 0 else block(i, h)
        return remote(src, block(i, h), up_s.at[i, s], up_r.at[i, s], above)

    def down(i, h, s):
        src = x_ref.at[i // parts, :, cols(i)] if s == 0 else block(i, h)
        return remote(src, block(i, h), down_s.at[i, s], down_r.at[i, s], below)

    def own(i):
        @pl.when(z < nz - 1)
        def _():
            up(i, z, 0).start()

        @pl.when(z > 0)
        def _():
            down(i, z, 0).start()

        here = pl.ds(pl.multiple_of(z * rows, rows), rows)
        gat[i // parts, here, cols(i)] = x_ref[i // parts, :, cols(i)]

    def hops(i):
        for s in range(1, nz):
            @pl.when(z - s >= 0)
            def _():
                up(i, z - s, s - 1).wait_recv()

            if s < nz - 1:
                @pl.when((z - s >= 0) & (z < nz - 1))
                def _():
                    up(i, z - s, s).start()

            @pl.when(z + s < nz)
            def _():
                down(i, z + s, s - 1).wait_recv()

            if s < nz - 1:
                @pl.when((z + s < nz) & (z > 0))
                def _():
                    down(i, z + s, s).start()

    def plane(i, k):
        peer = lax.rem(me + k, planes)
        theirs = pl.ds(pl.multiple_of(peer * slots, slots), slots)
        mine = pl.ds(pl.multiple_of(me * slots, slots), slots)
        return remote(
            stage.at[i // parts, theirs, cols(i)], recv.at[i // parts, mine, cols(i)],
            plane_s.at[i, k - 1], plane_r.at[i, k - 1], at_plane(peer, z, ny),
        )

    def pick(i):
        a = i // parts
        stage[a, :, cols(i)] = jnp.dot(
            pick_ref[...], gat[a, :, cols(i)], preferred_element_type=jnp.float32
        ).astype(jnp.bfloat16)

        def one(k, carry):
            plane(i, k).start()
            return carry

        lax.fori_loop(1, planes, one, 0)
        mine = pl.ds(pl.multiple_of(me * slots, slots), slots)
        recv[a, mine, cols(i)] = stage[a, mine, cols(i)]

    def finish(i):
        a = i // parts

        def one(k, carry):
            plane(i, k).wait_recv()
            return carry

        lax.fori_loop(1, planes, one, 0)
        out_ref[a, :, cols(i)] = jnp.dot(
            place_ref[...], recv[a, :, cols(i)], preferred_element_type=jnp.float32
        ).astype(jnp.bfloat16)

    own(0)
    own(1)

    def step(i, carry):
        @pl.when(i + 2 < items)
        def _():
            own(i + 2)

        hops(i)
        pick(i)

        @pl.when(i > 0)
        def _():
            finish(i - 1)

        return carry

    lax.fori_loop(0, items, step, 0)
    finish(items - 1)

    def drain(i, carry):
        for s in range(nz - 1):
            @pl.when((z - s >= 0) & (z < nz - 1))
            def _():
                up(i, z - s, s).wait_send()

            @pl.when((z + s < nz) & (z > 0))
            def _():
                down(i, z + s, s).wait_send()

        def one(k, c):
            plane(i, k).wait_send()
            return c

        return lax.fori_loop(1, planes, one, carry)

    lax.fori_loop(0, items, drain, 0)


def dispatch(x, picker, placer, nz, planes):
    _, rows, width = x.shape
    taken = placer.shape[1]
    cap = placer.shape[0]
    chunk = width // 4
    items = 2 * (width // chunk)
    dma = pltpu.SemaphoreType.DMA
    vmem = pl.BlockSpec(memory_space=pltpu.VMEM)
    return pl.pallas_call(
        functools.partial(dispatch_kernel, chunk),
        out_shape=jax.ShapeDtypeStruct((2, cap, width), jnp.bfloat16),
        in_specs=[vmem] * 3,
        out_specs=vmem,
        scratch_shapes=[
            pltpu.VMEM((2, nz * rows, width), jnp.bfloat16),
            pltpu.VMEM((2, taken, width), jnp.bfloat16),
            pltpu.VMEM((2, taken, width), jnp.bfloat16),
            dma((items, nz - 1)), dma((items, nz - 1)),
            dma((items, nz - 1)), dma((items, nz - 1)),
            dma((items, planes - 1)), dma((items, planes - 1)),
        ],
        compiler_params=pltpu.CompilerParams(
            collective_id=0, has_side_effects=True, vmem_limit_bytes=48 * 2**20
        ),
    )(x, picker, placer)


def collect_kernel(
    chunk, rg_ref, place_ref, pick_ref, og_ref, piece, stage, recv, part,
    from_down, from_up, to_down, to_up,
    plane_s, plane_r, rd_s, rd_r, ru_s, ru_r, up_s, up_r, down_s, down_r, y_s, y_r,
):
    groups, nz, ny, g, z, y = place()
    planes = groups * ny
    me = g * ny + y
    rows, width = og_ref.shape
    slots = stage.shape[0] // planes
    parts = width // chunk
    above = (g, (z + 1) * ny + y)
    below = (g, (z - 1) * ny + y)
    greet(g, z, y, nz, ny, planes)

    def cols(q):
        return pl.ds(pl.multiple_of(q * chunk, chunk), chunk)

    def line(h):
        return pl.ds(pl.multiple_of(h * rows, rows), rows)

    def plane(q, k):
        peer = lax.rem(me + k, planes)
        theirs = pl.ds(pl.multiple_of(peer * slots, slots), slots)
        mine = pl.ds(pl.multiple_of(me * slots, slots), slots)
        return remote(
            stage.at[theirs, cols(q)], recv.at[mine, cols(q)],
            plane_s.at[q, k - 1], plane_r.at[q, k - 1], at_plane(peer, z, ny),
        )

    def reduce_down(q, h):
        return remote(
            to_down.at[line(h), cols(q)], from_up.at[line(h), cols(q)],
            rd_s.at[q, h], rd_r.at[q, h], below,
        )

    def reduce_up(q, h):
        return remote(
            to_up.at[line(h), cols(q)], from_down.at[line(h), cols(q)],
            ru_s.at[q, h], ru_r.at[q, h], above,
        )

    def block(q, h, side):
        return piece.at[pl.ds(pl.multiple_of((h * ny + side) * rows, rows), rows), cols(q)]

    def up(q, h, s):
        return remote(block(q, h, y), block(q, h, y), up_s.at[q, s], up_r.at[q, s], above)

    def down(q, h, s):
        return remote(block(q, h, y), block(q, h, y), down_s.at[q, s], down_r.at[q, s], below)

    def sideways(q, h, k):
        side = lax.rem(y + k, ny)
        return remote(
            block(q, h, y), block(q, h, y), y_s.at[q, h, k - 1], y_r.at[q, h, k - 1],
            (g, z * ny + side),
        )

    def share(q, h):
        for k in range(1, ny):
            sideways(q, h, k).start()

    def scatter(q):
        stage[:, cols(q)] = jnp.dot(
            place_ref[...], rg_ref[:, cols(q)], preferred_element_type=jnp.float32
        ).astype(jnp.bfloat16)

        def one(k, carry):
            plane(q, k).start()
            return carry

        lax.fori_loop(1, planes, one, 0)
        mine = pl.ds(pl.multiple_of(me * slots, slots), slots)
        recv[mine, cols(q)] = stage[mine, cols(q)]

    def gathered(q):
        def one(k, carry):
            plane(q, k).wait_recv()
            return carry

        lax.fori_loop(1, planes, one, 0)
        part[:, cols(q)] = jnp.dot(
            pick_ref[...], recv[:, cols(q)], preferred_element_type=jnp.float32
        )

    def hop(q, h):
        @pl.when(z == nz - 1 - h)
        def _():
            for far in range(nz - 1 - h):
                total = part[line(far), cols(q)]
                if h > 0:
                    reduce_down(q, far).wait_recv()
                    total = total + from_up[line(far), cols(q)].astype(jnp.float32)
                to_down[line(far), cols(q)] = total.astype(jnp.bfloat16)
                reduce_down(q, far).start()

        @pl.when(z == h)
        def _():
            for far in range(nz - 1, h, -1):
                total = part[line(far), cols(q)]
                if h > 0:
                    reduce_up(q, far).wait_recv()
                    total = total + from_down[line(far), cols(q)].astype(jnp.float32)
                to_up[line(far), cols(q)] = total.astype(jnp.bfloat16)
                reduce_up(q, far).start()

    def total(q):
        here = line(z)

        @pl.when(z < nz - 1)
        def _():
            reduce_down(q, z).wait_recv()
            part[here, cols(q)] += from_up[here, cols(q)].astype(jnp.float32)

        @pl.when(z > 0)
        def _():
            reduce_up(q, z).wait_recv()
            part[here, cols(q)] += from_down[here, cols(q)].astype(jnp.float32)

        mine = pl.ds(pl.multiple_of((z * ny + y) * rows, rows), rows)
        piece[mine, cols(q)] = (
            og_ref[:, cols(q)].astype(jnp.float32) + part[here, cols(q)]
        ).astype(jnp.bfloat16)

        @pl.when(z < nz - 1)
        def _():
            up(q, z, 0).start()

        @pl.when(z > 0)
        def _():
            down(q, z, 0).start()

        share(q, z)

    def forward(q, s):
        @pl.when(z - s >= 0)
        def _():
            up(q, z - s, s - 1).wait_recv()
            if s < nz - 1:
                @pl.when(z < nz - 1)
                def _():
                    up(q, z - s, s).start()
            share(q, z - s)

        @pl.when(z + s < nz)
        def _():
            down(q, z + s, s - 1).wait_recv()
            if s < nz - 1:
                @pl.when(z > 0)
                def _():
                    down(q, z + s, s).start()
            share(q, z + s)

    stages = [scatter, gathered]
    stages += [functools.partial(lambda h, q: hop(q, h), h) for h in range(nz - 1)]
    stages += [total]
    stages += [functools.partial(lambda s, q: forward(q, s), s) for s in range(1, nz)]

    def step(t, carry):
        for k in reversed(range(len(stages))):
            @pl.when((t >= k) & (t - k < parts))
            def _():
                stages[k](t - k)

        return carry

    lax.fori_loop(0, parts + len(stages) - 1, step, 0)

    def drain(q, carry):
        def one(k, c):
            plane(q, k).wait_send()
            return c

        lax.fori_loop(1, planes, one, 0)
        for h in range(nz):
            @pl.when(h < z)
            def _():
                reduce_down(q, h).wait_send()

            @pl.when(h > z)
            def _():
                reduce_up(q, h).wait_send()

            for k in range(1, ny):
                side = lax.rem(y + ny - k, ny)
                remote(
                    block(q, h, y), block(q, h, side), y_s.at[q, h, k - 1],
                    y_r.at[q, h, k - 1], (g, z * ny + side),
                ).wait()
        for s in range(nz - 1):
            @pl.when((z - s >= 0) & (z < nz - 1))
            def _():
                up(q, z - s, s).wait_send()

            @pl.when((z + s < nz) & (z > 0))
            def _():
                down(q, z + s, s).wait_send()

        return carry

    lax.fori_loop(0, parts, drain, 0)


def collect(row_grad, placer, picker, out_grad, nz, ny, planes):
    rows, width = out_grad.shape
    taken = placer.shape[0]
    chunk = width // 4
    parts = width // chunk
    dma = pltpu.SemaphoreType.DMA
    vmem = pl.BlockSpec(memory_space=pltpu.VMEM)
    line = (nz * rows, width)
    return pl.pallas_call(
        functools.partial(collect_kernel, chunk),
        out_shape=jax.ShapeDtypeStruct((nz * ny * rows, width), jnp.bfloat16),
        in_specs=[vmem] * 4,
        out_specs=vmem,
        scratch_shapes=[
            pltpu.VMEM((taken, width), jnp.bfloat16),
            pltpu.VMEM((taken, width), jnp.bfloat16),
            pltpu.VMEM(line, jnp.float32),
            pltpu.VMEM(line, jnp.bfloat16),
            pltpu.VMEM(line, jnp.bfloat16),
            pltpu.VMEM(line, jnp.bfloat16),
            pltpu.VMEM(line, jnp.bfloat16),
            dma((parts, planes - 1)), dma((parts, planes - 1)),
            dma((parts, nz)), dma((parts, nz)),
            dma((parts, nz)), dma((parts, nz)),
            dma((parts, nz - 1)), dma((parts, nz - 1)),
            dma((parts, nz - 1)), dma((parts, nz - 1)),
            dma((parts, nz, ny - 1)), dma((parts, nz, ny - 1)),
        ],
        compiler_params=pltpu.CompilerParams(
            collective_id=1, has_side_effects=True, vmem_limit_bytes=48 * 2**20
        ),
    )(row_grad, placer, picker, out_grad)


def expert_backward(rows_in, rows_grad, scales, gate_w, up_w, down_w):
    gate_pre = jnp.dot(rows_in, gate_w, preferred_element_type=jnp.float32)
    up_pre = jnp.dot(rows_in, up_w, preferred_element_type=jnp.float32)
    sig = jax.nn.sigmoid(gate_pre)
    silu = gate_pre * sig
    hidden = (silu * up_pre).astype(jnp.bfloat16)
    scaled = (rows_grad.astype(jnp.float32) * scales[:, None]).astype(jnp.bfloat16)
    outer = (((0,), (0,)), ((), ()))
    inner_dims = (((1,), (1,)), ((), ()))
    back_hidden = lax.dot_general(scaled, down_w, inner_dims, preferred_element_type=jnp.float32)
    back_gate = (back_hidden * up_pre * sig * (1.0 + gate_pre * (1.0 - sig))).astype(jnp.bfloat16)
    back_up = (back_hidden * silu).astype(jnp.bfloat16)
    row_grad = lax.dot_general(back_gate, gate_w, inner_dims, preferred_element_type=jnp.float32)
    row_grad = row_grad + lax.dot_general(
        back_up, up_w, inner_dims, preferred_element_type=jnp.float32
    )
    grad_down = lax.dot_general(hidden, scaled, outer, preferred_element_type=jnp.float32).astype(
        jnp.bfloat16
    )
    grad_gate = lax.dot_general(
        rows_in, back_gate, outer, preferred_element_type=jnp.float32
    ).astype(jnp.bfloat16)
    grad_up = lax.dot_general(rows_in, back_up, outer, preferred_element_type=jnp.float32).astype(
        jnp.bfloat16
    )
    return (grad_gate, grad_up, grad_down, row_grad.astype(jnp.bfloat16))


def tables(selected, rows, most):
    groups, nz, ny, g, z, y = place()
    inner = nz * ny
    planes = groups * ny
    cap = selected.shape[1]
    me = g * ny + y
    experts = selected.reshape(groups, nz, ny, cap)
    experts = lax.dynamic_index_in_dim(experts, z, 1, keepdims=False).reshape(planes, cap)
    owner = experts // rows
    owner_z = (owner % inner) // ny
    owner_p = (owner // inner) * ny + owner % ny
    slot_range = jnp.arange(cap, dtype=jnp.int32)
    earlier = (owner[:, :, None] == owner[:, None, :]) & (
        slot_range[None, :, None] > slot_range[None, None, :]
    )
    ranking = jnp.sum(earlier.astype(jnp.int32), axis=2)
    slots = nz * most
    slot = owner_z * most + ranking
    token = owner_z * rows + experts % rows
    hit = (owner_p == me)[:, :, None] & (
        slot[:, :, None] == jnp.arange(slots, dtype=jnp.int32)[None, None, :]
    )
    table = jnp.sum(jnp.where(hit, token[:, :, None] + 1, 0), axis=1).reshape(-1)
    token_ids = jnp.arange(nz * rows, dtype=jnp.int32) + 1
    picker = (table[:, None] == token_ids[None, :]).astype(jnp.bfloat16)
    position = lax.dynamic_index_in_dim(owner_p * slots + slot, me, 0, keepdims=False)
    arrival = jnp.arange(planes * slots, dtype=jnp.int32)
    placer = (position[:, None] == arrival[None, :]).astype(jnp.bfloat16)
    return picker, placer


def body(moe_input, out_grad, context, gate_scale, selected, w_gate, w_up, w_down, w_out):
    groups = lax.axis_size("grp")
    inner_count = lax.axis_size("inner")
    devices = groups * inner_count
    nz, ny = split_inner(inner_count)
    planes = groups * ny
    tok_rows, width = moe_input.shape
    capacity = selected.shape[1]
    most = max(4, (2 * capacity + devices - 1) // devices)
    picker, placer = tables(selected, tok_rows, most)
    rows = dispatch(jnp.stack([moe_input, out_grad]), picker, placer, nz, planes)
    grad_gate, grad_up, grad_down, row_grad = expert_backward(
        rows[0], rows[1], gate_scale[0], w_gate[0], w_up[0], w_down[0]
    )
    piece = collect(row_grad, placer.T, picker.T, out_grad, nz, ny, planes)
    grad_ctx = lax.dot_general(
        piece, w_out, (((1,), (1,)), ((), ())), preferred_element_type=jnp.float32
    )
    grad_proj = lax.dot_general(
        context, piece, (((0,), (0,)), ((), ())), preferred_element_type=jnp.float32
    )
    proj_share = lax.psum_scatter(
        grad_proj.astype(jnp.bfloat16), "grp", scatter_dimension=1, tiled=True
    )
    return (
        grad_gate[None],
        grad_up[None],
        grad_down[None],
        grad_ctx.astype(jnp.bfloat16),
        proj_share,
    )


def solution(mesh):
    placed = (
        P(("grp", "inner"), None),
        P(("grp", "inner"), None),
        P("grp", "inner"),
        P(("grp", "inner"), None),
        P(),
        P(("grp", "inner"), None, None),
        P(("grp", "inner"), None, None),
        P(("grp", "inner"), None, None),
        P("inner", None),
    )
    return jax.shard_map(
        body,
        mesh=mesh,
        in_specs=placed,
        out_specs=(
            P(("grp", "inner"), None, None),
            P(("grp", "inner"), None, None),
            P(("grp", "inner"), None, None),
            P("grp", "inner"),
            P("inner", "grp"),
        ),
        check_vma=False,
    )
```

time: 310 us -> 238 us (0.77)
  Pallas kernels: 0 us -> 172 us
  waiting for transfers between devices: 177 us -> 16.2 us
  blocking collectives: 52.9 us -> 0 us
  matrix products: 46.2 us -> 24.1 us
  starting transfers between devices: 11.2 us -> 0.04 us
  local copies, waits for them, and re-layouts: 3.87 us -> 7.61 us
    pallas_call x0 -> x2, Pallas kernels: none -> 172 us  [the longest x1 86.4 us: collect(): pl.pallas_call(functools.partial(collect_kernel, chunk), out_shape=jax.Sh...]
    all_to_all x2 -> x0, waiting for transfers between devices: 90.4 us -> none  [the longest x1 46.9 us: body(): lax.all_to_all(send_input, ('grp', 'inner'), split_axis=0, concat_axis=0,...]
    all_gather x1 -> x0, waiting for transfers between devices: 70.9 us -> none  [body(): piece = lax.all_gather(total, 'inner', axis=0, tiled=True)]
    all_to_all x1 -> x0, blocking collectives: 52.9 us -> none  [body(): lax.all_to_all(placed.reshape(devices, most, width), ('grp', 'inner'), sp...]
    dot_general x6 -> x1, matrix products: 17.3 us -> 1.01 us  [expert_backward(): lax.dot_general(back_up, up_w, inner_dims, preferred_element_type=jnp.flo...]
    all_to_all x2 -> x0, starting transfers between devices: 10.9 us -> none  [the longest x1 7.43 us: body(): lax.all_to_all(send_input, ('grp', 'inner'), split_axis=0, concat_axis=0,...]
    unnamed x29 -> x40, local copies, waits for them, and re-layouts: 3.5 us -> 6.6 us
  transfers between devices with their start and end apart: 4 -> 1, of which waited for: 4 -> 1; matrix products, arithmetic and copies ran while one was open for 7% -> 5% of each run, Pallas kernels for 0% -> 0%
where the time goes in v1:
time: 238 us
  Pallas kernels  172 us (72%)
  matrix products  24.1 us (10%)
  waiting for transfers between devices  16.2 us (7%)
  between operations  14.4 us (6%)
  local copies, waits for them, and re-layouts  7.61 us (3%)
  other arithmetic  3.52 us (1%)
    pallas_call x1, Pallas kernels, collect(): pl.pallas_call(functools.partial(collect_kernel, chunk), out_shape=jax.Sh...  86.4 us
    pallas_call x1, Pallas kernels, dispatch(): pl.pallas_call(functools.partial(dispatch_kernel, chunk), out_shape=jax.S...  85.4 us
    reduce_scatter x1, waiting for transfers between devices, body(): lax.psum_scatter(grad_proj.astype(jnp.bfloat16), 'grp', scatter_dimension...  16.2 us
    unnamed x40, local copies, waits for them, and re-layouts  6.6 us
    dot_general x1, matrix products, body(): lax.dot_general(context, piece, (((0,), (0,)), ((), ())), preferred_eleme...  5.97 us
  transfers between devices with their start and end apart: 1, of which 1 were waited for; matrix products, arithmetic and copies ran while one was open for 5% of the time, Pallas kernels for 0%

profile of v1, /device:TPU:0, one launch (start us, length us, event | category | flops | bytes accessed | tf_op | source)
XLA Modules:
  0.0 237.7 jit_solution(9882125888629895102)
XLA Ops:
  7.2 0.0 copy-start
  7.2 0.0 reduce-scatter.2.cloned.1.call-start
  7.3 0.9 reshape.215
  8.3 0.8 convert_reduce_fusion
  9.2 0.1 fusion.41.place_ref
  9.2 0.8 fusion.40.place_ref
  10.1 0.2 select_reduce_fusion
  10.3 0.1 eq.94
  10.4 0.0 copy-start.4
  10.4 0.2 compare_convert_fusion
  10.6 1.3 pad_maximum_fusion.x_ref
  11.9 0.0 copy-done.4
  11.9 85.4 %shard_map.131 = bf16[2,256,2048]{2,1,0:T(8,128)(2,1)S(1)} custom-call(bf16[2,128,2048]{2,1,0:T(8,128)(2,1)S(1)} %pad_maximum_fusion.x_ref, bf16[512,512]{1,0:T(8,128)(2,1)S(1)} %get-tuple-element.22.pick_ref, bf16[256,512]{1,0:T(8,128)(2,1)S(1)} %copy-done.4), custom_call_target="tpu_custom_call" | custom-call | tf_op jit(solution)/shard_map/pallas_call | solution.py:206
  97.4 0.0 copy-done
  97.4 0.0 copy-start.2
  97.4 0.0 copy-start.6
  97.4 1.0 fusion.2
  98.4 1.7 copy-done.6
  100.1 0.0 copy-start.15
  100.1 0.0 copy-start.11
  100.1 0.0 copy-start.14
  100.1 1.0 fusion.6
  101.0 0.0 copy-start.17
  101.0 0.0 copy-done.2
  101.1 1.5 copy-done.11
  102.5 0.0 copy-done.14
  102.5 1.2 multiply_convert_fusion.1
  103.7 0.0 copy-done.15
  103.7 0.0 copy-done.17
  103.8 0.0 copy-start.9
  103.8 0.0 copy-start.7
  103.8 1.0 fusion
  104.8 0.0 copy-done.9
  104.8 0.0 copy-start.1
  104.8 1.0 fusion.17.rg_ref
  105.8 0.0 copy-done.7
  105.8 0.0 copy-done.1
  105.8 0.0 copy-start.13
  105.9 86.4 %shard_map.132 = bf16[1024,2048]{1,0:T(8,128)(2,1)} custom-call(bf16[256,2048]{1,0:T(8,128)(2,1)S(1)} %fusion.17.rg_ref, bf16[512,256]{1,0:T(8,128)(2,1)S(1)} %fusion.41.place_ref, bf16[512,512]{1,0:T(8,128)(2,1)S(1)} %get-tuple-element.21.pick_ref, bf16[128,2048]{1,0:T(8,128)(2,1)S(1)} %copy-done.1), custom_call_target="tpu_custom_call" | custom-call | tf_op jit(solution)/shard_map/pallas_call | solution.py:436
  192.2 0.0 copy-done.13
  192.3 0.0 copy-start.8
  192.3 6.0 %fusion.16 = bf16[512,2048]{0,1:T(8,128)(2,1)} fusion(bf16[1024,2048]{1,0:T(8,128)(2,1)} %shard_map.132, bf16[1024,512]{1,0:T(8,128)(2,1)S(1)} %copy-done.13), kind=kOutput, calls=%fused_computation.18 | convolution fusion | flops 2148532224 | bytes 7340032 | tf_op jit(solution)/shard_map/dot_general | solution.py:539
  198.2 0.0 reduce-scatter.2.cloned.1.call-update
  198.3 0.0 copy-done.8
  198.3 0.0 copy-start.3
  198.3 0.0 copy-start.10
  198.3 4.1 %fusion.11 = bf16[1,2048,768]{2,1,0:T(8,128)(2,1)} fusion(bf16[256,768]{1,0:T(8,128)(2,1)S(1)} %copy-done.8, bf16[2,256,2048]{2,1,0:T(8,128)(2,1)} %copy-done.2), kind=kOutput, calls=%fused_computation.15 | convolution fusion | flops 806879232 | bytes 4587520 | tf_op jit(solution)/shard_map/dot_general | solution.py:484
  202.4 0.0 copy-done.3
  202.4 0.0 copy-done.10
  202.4 0.0 copy-start.16
  202.4 0.0 copy-start.18
  202.4 2.7 %fusion.10 = bf16[1,2048,768]{2,1,0:T(8,128)(2,1)} fusion(bf16[256,768]{1,0:T(8,128)(2,1)S(1)} %copy-done.10, bf16[2,256,2048]{2,1,0:T(8,128)(2,1)S(1)} %copy-done.3), kind=kOutput, calls=%fused_computation.14 | convolution fusion | flops 806879232 | bytes 4587520 | tf_op jit(solution)/shard_map/dot_general | solution.py:481
  205.1 0.0 copy-done.16
  205.1 0.0 copy-done.18
  205.1 0.0 copy-start.5
  205.1 0.0 copy-start.12
  205.1 2.9 %fusion.12 = bf16[1,768,2048]{2,1,0:T(8,128)(2,1)} fusion(f32[256]{0:T(256)S(1)} %bitcast.69, bf16[2,256,2048]{2,1,0:T(8,128)(2,1)S(1)} %copy-done.3, f32[256,768]{1,0:T(8,128)S(1)} %copy-done.18, f32[256,768]{1,0:T(8,128)S(1)} %copy-done.16), kind=kOutput, calls=%fused_computation.16 | convolution fusion | flops 809631744 | bytes 5768192 | tf_op jit(solution)/shard_map/dot_general | solution.py:478
  207.9 0.2 copy-done.5
  208.1 1.2 copy-done.12
  209.3 3.3 %convolution_convert_fusion.4 = bf16[1024,512]{1,0:T(8,128)(2,1)} fusion(bf16[1024,2048]{1,0:T(8,128)(2,1)S(1)} %copy-done.5, bf16[512,2048]{1,0:T(8,128)(2,1)S(1)} %copy-done.12), kind=kOutput, calls=%fused_computation.26 | convolution fusion | flops 2148007936 | bytes 7340032 | tf_op jit(solution)/shard_map/dot_general | solution.py:536
  212.6 16.2 %reduce-scatter.2.cloned.1.call-done = bf16[512,512]{0,1:T(8,128)(2,1)} async-done(((bf16[512,2048]{0,1:T(8,128)(2,1)}), bf16[512,512]{0,1:T(8,128)(2,1)}) %reduce-scatter.2.cloned.1.call-update) | async-done | bytes 524304 | tf_op jit(solution)/shard_map/reduce_scatter | solution.py:542
  228.8 2.0 copy.16
  (8 shorter events, 0.1 us)
Async XLA Ops:
  7.2 90.2 %copy-start = (bf16[1,2048,768]{2,1,0:T(8,128)(2,1)S(1)}, bf16[1,2048,768]{2,1,0:T(8,128)(2,1)}, u32[]{:S(2)}) copy-start(bf16[1,2048,768]{2,1,0:T(8,128)(2,1)} %param.14) | copy-start | bytes 9437188
  7.2 221.6 %reduce-scatter.2.cloned.1.call-start = ((), (), s32[]{:S(2)}) async-start(), calls=%async_computation.1 | async-start | bytes 2621440 | tf_op jit(solution)/shard_map/reduce_scatter | solution.py:542
  10.4 1.6 copy-start.4
  97.4 3.7 %copy-start.2 = (bf16[2,256,2048]{2,1,0:T(8,128)(2,1)}, bf16[2,256,2048]{2,1,0:T(8,128)(2,1)S(1)}, u32[]{:S(2)}) copy-start(bf16[2,256,2048]{2,1,0:T(8,128)(2,1)S(1)} %shard_map.131) | copy-start | bytes 6291460
  97.4 2.6 %copy-start.6 = (bf16[1,2048,768]{2,1,0:T(8,128)(2,1)S(1)}, bf16[1,2048,768]{2,1,0:T(8,128)(2,1)}, u32[]{:S(2)}) copy-start(bf16[1,2048,768]{2,1,0:T(8,128)(2,1)} %param.15) | copy-start | bytes 9437188
  100.1 3.7 %copy-start.15 = (f32[256,768]{1,0:T(8,128)}, f32[256,768]{1,0:T(8,128)S(1)}, u32[]{:S(2)}) copy-start(f32[256,768]{1,0:T(8,128)S(1)} %fusion.2) | copy-start | bytes 2359300
  100.1 2.5 %copy-start.11 = (bf16[1,768,2048]{2,1,0:T(8,128)(2,1)S(1)}, bf16[1,768,2048]{2,1,0:T(8,128)(2,1)}, u32[]{:S(2)}) copy-start(bf16[1,768,2048]{2,1,0:T(8,128)(2,1)} %param.16) | copy-start | bytes 9437188
  100.1 2.5 %copy-start.14 = (f32[1,256]{1,0:T(1,128)S(1)}, f32[1,256]{1,0:T(1,128)}, u32[]{:S(2)}) copy-start(f32[1,256]{1,0:T(1,128)} %param.12) | copy-start | bytes 3076
  101.0 2.7 %copy-start.17 = (f32[256,768]{1,0:T(8,128)}, f32[256,768]{1,0:T(8,128)S(1)}, u32[]{:S(2)}) copy-start(f32[256,768]{1,0:T(8,128)S(1)} %fusion.6) | copy-start | bytes 2359300
  103.8 1.0 copy-start.9
  103.8 2.1 copy-start.7
  104.8 1.0 copy-start.1
  105.8 86.4 %copy-start.13 = (bf16[1024,512]{1,0:T(8,128)(2,1)S(1)}, bf16[1024,512]{1,0:T(8,128)(2,1)}, u32[]{:S(2)}) copy-start(bf16[1024,512]{1,0:T(8,128)(2,1)} %param.11) | copy-start | bytes 3145732
  192.3 6.0 %copy-start.8 = (bf16[256,768]{1,0:T(8,128)(2,1)S(1)}, bf16[256,768]{1,0:T(8,128)(2,1)}, u32[]{:S(2)}) copy-start(bf16[256,768]{1,0:T(8,128)(2,1)} %copy-done.7) | copy-start | bytes 1179652
  198.3 4.1 %copy-start.3 = (bf16[2,256,2048]{2,1,0:T(8,128)(2,1)S(1)}, bf16[2,256,2048]{2,1,0:T(8,128)(2,1)}, u32[]{:S(2)}) copy-start(bf16[2,256,2048]{2,1,0:T(8,128)(2,1)} %copy-done.2) | copy-start | bytes 6291460
  198.3 4.1 %copy-start.10 = (bf16[256,768]{1,0:T(8,128)(2,1)S(1)}, bf16[256,768]{1,0:T(8,128)(2,1)}, u32[]{:S(2)}) copy-start(bf16[256,768]{1,0:T(8,128)(2,1)} %copy-done.9) | copy-start | bytes 1179652
  202.4 2.7 %copy-start.16 = (f32[256,768]{1,0:T(8,128)S(1)}, f32[256,768]{1,0:T(8,128)}, u32[]{:S(2)}) copy-start(f32[256,768]{1,0:T(8,128)} %copy-done.15) | copy-start | bytes 2359300
  202.4 2.7 %copy-start.18 = (f32[256,768]{1,0:T(8,128)S(1)}, f32[256,768]{1,0:T(8,128)}, u32[]{:S(2)}) copy-start(f32[256,768]{1,0:T(8,128)} %copy-done.17) | copy-start | bytes 2359300
  205.1 3.0 %copy-start.5 = (bf16[1024,2048]{1,0:T(8,128)(2,1)S(1)}, bf16[1024,2048]{1,0:T(8,128)(2,1)}, u32[]{:S(2)}) copy-start(bf16[1024,2048]{1,0:T(8,128)(2,1)} %shard_map.132) | copy-start | bytes 12582916
  205.1 4.2 %copy-start.12 = (bf16[512,2048]{1,0:T(8,128)(2,1)S(1)}, bf16[512,2048]{1,0:T(8,128)(2,1)}, u32[]{:S(2)}) copy-start(bf16[512,2048]{1,0:T(8,128)(2,1)} %param.17) | copy-start | bytes 6291460
Sparse Core Ops, SparseCore 0:
  198.4 30.3 reduce-scatter.1

commit v2 on v1

--- a/solution.py
+++ b/solution.py
@@ -199,7 +199,7 @@
     _, rows, width = x.shape
     taken = placer.shape[1]
     cap = placer.shape[0]
-    chunk = width // 4
+    chunk = width // 8
     items = 2 * (width // chunk)
     dma = pltpu.SemaphoreType.DMA
     vmem = pl.BlockSpec(memory_space=pltpu.VMEM)
@@ -267,11 +267,57 @@
     def block(q, h, side):
         return piece.at[pl.ds(pl.multiple_of((h * ny + side) * rows, rows), rows), cols(q)]
 
-    def up(q, h, s):
-        return remote(block(q, h, y), block(q, h, y), up_s.at[q, s], up_r.at[q, s], above)
-
-    def down(q, h, s):
-        return remote(block(q, h, y), block(q, h, y), down_s.at[q, s], down_r.at[q, s], below)
+    def up(q, h, s, k=0):
+        this = block(q, h, lax.rem(y + k, ny))
+        return remote(this, this, up_s.at[q, k, s], up_r.at[q, k, s], above)
+
+    def down(q, h, s, k=0):
+        this = block(q, h, lax.rem(y + k, ny))
+        return remote(this, this, down_s.at[q, k, s], down_r.at[q, k, s], below)
+
+    def sideways_first(q):
+        return q % 4 == 1
+
+    def beside(q, h, k):
+        side = lax.rem(y + k, ny)
+        return remote(
+            block(q, h, y), block(q, h, side), y_s.at[q, h, ny - 1 - k],
+            y_r.at[q, h, ny - 1 - k], (g, z * ny + side),
+        )
+
+    def leave(q, k):
+        @pl.when(z < nz - 1)
+        def _():
+            up(q, z, 0, k).start()
+
+        @pl.when(z > 0)
+        def _():
+            down(q, z, 0, k).start()
+
+    def along(q, s, k):
+        @pl.when(z - s >= 0)
+        def _():
+            up(q, z - s, s - 1, k).wait_recv()
+            if s < nz - 1:
+                @pl.when(z < nz - 1)
+                def _():
+                    up(q, z - s, s, k).start()
+            if k == 0:
+                @pl.when(jnp.logical_not(sideways_first(q)))
+                def _():
+                    share(q, z - s)
+
+        @pl.when(z + s < nz)
+        def _():
+            down(q, z + s, s - 1, k).wait_recv()
+            if s < nz - 1:
+                @pl.when(z > 0)
+                def _():
+                    down(q, z + s, s, k).start()
+            if k == 0:
+                @pl.when(jnp.logical_not(sideways_first(q)))
+                def _():
+                    share(q, z + s)
 
     def sideways(q, h, k):
         side = lax.rem(y + k, ny)
@@ -346,39 +392,26 @@
             og_ref[:, cols(q)].astype(jnp.float32) + part[here, cols(q)]
         ).astype(jnp.bfloat16)
 
-        @pl.when(z < nz - 1)
-        def _():
-            up(q, z, 0).start()
-
-        @pl.when(z > 0)
-        def _():
-            down(q, z, 0).start()
-
+        leave(q, 0)
         share(q, z)
 
     def forward(q, s):
-        @pl.when(z - s >= 0)
-        def _():
-            up(q, z - s, s - 1).wait_recv()
-            if s < nz - 1:
-                @pl.when(z < nz - 1)
-                def _():
-                    up(q, z - s, s).start()
-            share(q, z - s)
-
-        @pl.when(z + s < nz)
-        def _():
-            down(q, z + s, s - 1).wait_recv()
-            if s < nz - 1:
-                @pl.when(z > 0)
-                def _():
-                    down(q, z + s, s).start()
-            share(q, z + s)
+        if s < nz:
+            along(q, s, 0)
+
+        @pl.when(sideways_first(q))
+        def _():
+            for k in range(1, ny):
+                if s == 1:
+                    beside(q, z, k).wait_recv()
+                    leave(q, k)
+                else:
+                    along(q, s - 1, k)
 
     stages = [scatter, gathered]
     stages += [functools.partial(lambda h, q: hop(q, h), h) for h in range(nz - 1)]
     stages += [total]
-    stages += [functools.partial(lambda s, q: forward(q, s), s) for s in range(1, nz)]
+    stages += [functools.partial(lambda s, q: forward(q, s), s) for s in range(1, nz + 1)]
 
     def step(t, carry):
         for k in reversed(range(len(stages))):
@@ -405,20 +438,26 @@
             def _():
                 reduce_up(q, h).wait_send()
 
+            shared = jnp.logical_or(h == z, jnp.logical_not(sideways_first(q)))
             for k in range(1, ny):
-                side = lax.rem(y + ny - k, ny)
-                remote(
-                    block(q, h, y), block(q, h, side), y_s.at[q, h, k - 1],
-                    y_r.at[q, h, k - 1], (g, z * ny + side),
-                ).wait()
+                @pl.when(shared)
+                def _():
+                    sideways(q, h, k).wait_send()
+
+                @pl.when(jnp.logical_not(sideways_first(q)))
+                def _():
+                    beside(q, h, k).wait_recv()
         for s in range(nz - 1):
-            @pl.when((z - s >= 0) & (z < nz - 1))
-            def _():
-                up(q, z - s, s).wait_send()
-
-            @pl.when((z + s < nz) & (z > 0))
-            def _():
-                down(q, z + s, s).wait_send()
+            for k in range(ny):
+                used = sideways_first(q) if k else (z >= 0)
+
+                @pl.when(used & (z - s >= 0) & (z < nz - 1))
+                def _():
+                    up(q, z - s, s, k).wait_send()
+
+                @pl.when(used & (z + s < nz) & (z > 0))
+                def _():
+                    down(q, z + s, s, k).wait_send()
 
         return carry
 
@@ -428,7 +467,7 @@
 def collect(row_grad, placer, picker, out_grad, nz, ny, planes):
     rows, width = out_grad.shape
     taken = placer.shape[0]
-    chunk = width // 4
+    chunk = width // 8
     parts = width // chunk
     dma = pltpu.SemaphoreType.DMA
     vmem = pl.BlockSpec(memory_space=pltpu.VMEM)
@@ -449,8 +488,8 @@
             dma((parts, planes - 1)), dma((parts, planes - 1)),
             dma((parts, nz)), dma((parts, nz)),
             dma((parts, nz)), dma((parts, nz)),
-            dma((parts, nz - 1)), dma((parts, nz - 1)),
-            dma((parts, nz - 1)), dma((parts, nz - 1)),
+            dma((parts, ny, nz - 1)), dma((parts, ny, nz - 1)),
+            dma((parts, ny, nz - 1)), dma((parts, ny, nz - 1)),
             dma((parts, nz, ny - 1)), dma((parts, nz, ny - 1)),
         ],
         compiler_params=pltpu.CompilerParams(

time: 238 us -> 254 us (1.067)
  Pallas kernels: 172 us -> 189 us
    pallas_call x1, Pallas kernels: 85.4 us -> 95.7 us  [dispatch(): pl.pallas_call(functools.partial(dispatch_kernel, chunk), out_shape=jax.S...]
    pallas_call x1, Pallas kernels: 86.4 us -> 93 us  [collect(): pl.pallas_call(functools.partial(collect_kernel, chunk), out_shape=jax.Sh...]
where the time goes in v2:
time: 254 us; the launch traced here: 253 us
  Pallas kernels  189 us (74%)
  matrix products  24.1 us (9%)
  waiting for transfers between devices  15 us (6%)
  between operations  14.4 us (6%)
  local copies, waits for them, and re-layouts  7.45 us (3%)
  other arithmetic  3.52 us (1%)
    pallas_call x1, Pallas kernels, dispatch(): pl.pallas_call(functools.partial(dispatch_kernel, chunk), out_shape=jax.S...  95.7 us
    pallas_call x1, Pallas kernels, collect(): pl.pallas_call(functools.partial(collect_kernel, chunk), out_shape=jax.Sh...  93 us
    reduce_scatter x1, waiting for transfers between devices, body(): lax.psum_scatter(grad_proj.astype(jnp.bfloat16), 'grp', scatter_dimension...  15 us
    unnamed x40, local copies, waits for them, and re-layouts  6.43 us
    dot_general x1, matrix products, body(): lax.dot_general(context, piece, (((0,), (0,)), ((), ())), preferred_eleme...  5.97 us
  transfers between devices with their start and end apart: 1, of which 1 were waited for; matrix products, arithmetic and copies ran while one was open for 5% of the time, Pallas kernels for 0%

profile of v2, /device:TPU:0, one launch (start us, length us, event | category | flops | bytes accessed | tf_op | source)
XLA Modules:
  0.0 253.3 jit_solution(15721109784416187449)
XLA Ops:
  7.2 0.0 copy-start
  7.2 0.0 reduce-scatter.2.cloned.1.call-start
  7.3 0.9 reshape.215
  8.3 0.8 convert_reduce_fusion
  9.2 0.1 fusion.41.place_ref
  9.2 0.8 fusion.40.place_ref
  10.1 0.2 select_reduce_fusion
  10.3 0.1 eq.94
  10.4 0.0 copy-start.4
  10.4 0.2 compare_convert_fusion
  10.6 1.3 pad_maximum_fusion.x_ref
  11.9 0.0 copy-done.4
  11.9 95.7 %shard_map.131 = bf16[2,256,2048]{2,1,0:T(8,128)(2,1)S(1)} custom-call(bf16[2,128,2048]{2,1,0:T(8,128)(2,1)S(1)} %pad_maximum_fusion.x_ref, bf16[512,512]{1,0:T(8,128)(2,1)S(1)} %get-tuple-element.22.pick_ref, bf16[256,512]{1,0:T(8,128)(2,1)S(1)} %copy-done.4), custom_call_target="tpu_custom_call" | custom-call | tf_op jit(solution)/shard_map/pallas_call | solution.py:206
  107.7 0.0 copy-done
  107.7 0.0 copy-start.2
  107.7 0.0 copy-start.6
  107.7 1.0 fusion.2
  108.7 1.7 copy-done.6
  110.3 0.0 copy-start.15
  110.3 0.0 copy-start.11
  110.3 0.0 copy-start.14
  110.3 1.0 fusion.6
  111.3 0.0 copy-start.17
  111.3 0.0 copy-done.2
  111.3 1.4 copy-done.11
  112.8 0.0 copy-done.14
  112.8 1.2 multiply_convert_fusion.1
  114.0 0.0 copy-done.15
  114.0 0.0 copy-done.17
  114.0 0.0 copy-start.9
  114.1 0.0 copy-start.7
  114.1 1.0 fusion
  115.1 0.0 copy-done.9
  115.1 0.0 copy-start.1
  115.1 1.0 fusion.17.rg_ref
  116.1 0.0 copy-done.7
  116.1 0.0 copy-done.1
  116.1 0.0 copy-start.13
  116.2 93.0 %shard_map.132 = bf16[1024,2048]{1,0:T(8,128)(2,1)} custom-call(bf16[256,2048]{1,0:T(8,128)(2,1)S(1)} %fusion.17.rg_ref, bf16[512,256]{1,0:T(8,128)(2,1)S(1)} %fusion.41.place_ref, bf16[512,512]{1,0:T(8,128)(2,1)S(1)} %get-tuple-element.21.pick_ref, bf16[128,2048]{1,0:T(8,128)(2,1)S(1)} %copy-done.1), custom_call_target="tpu_custom_call" | custom-call | tf_op jit(solution)/shard_map/pallas_call | solution.py:475
  209.2 0.0 copy-done.13
  209.2 0.0 copy-start.8
  209.2 6.0 %fusion.16 = bf16[512,2048]{0,1:T(8,128)(2,1)} fusion(bf16[1024,2048]{1,0:T(8,128)(2,1)} %shard_map.132, bf16[1024,512]{1,0:T(8,128)(2,1)S(1)} %copy-done.13), kind=kOutput, calls=%fused_computation.18 | convolution fusion | flops 2148532224 | bytes 7340032 | tf_op jit(solution)/shard_map/dot_general | solution.py:578
  215.2 0.0 reduce-scatter.2.cloned.1.call-update
  215.2 0.0 copy-done.8
  215.2 0.0 copy-start.3
  215.2 0.0 copy-start.10
  215.2 4.1 %fusion.11 = bf16[1,2048,768]{2,1,0:T(8,128)(2,1)} fusion(bf16[256,768]{1,0:T(8,128)(2,1)S(1)} %copy-done.8, bf16[2,256,2048]{2,1,0:T(8,128)(2,1)} %copy-done.2), kind=kOutput, calls=%fused_computation.15 | convolution fusion | flops 806879232 | bytes 4587520 | tf_op jit(solution)/shard_map/dot_general | solution.py:523
  219.3 0.0 copy-done.3
  219.3 0.0 copy-done.10
  219.3 0.0 copy-start.16
  219.3 0.0 copy-start.18
  219.3 2.7 %fusion.10 = bf16[1,2048,768]{2,1,0:T(8,128)(2,1)} fusion(bf16[256,768]{1,0:T(8,128)(2,1)S(1)} %copy-done.10, bf16[2,256,2048]{2,1,0:T(8,128)(2,1)S(1)} %copy-done.3), kind=kOutput, calls=%fused_computation.14 | convolution fusion | flops 806879232 | bytes 4587520 | tf_op jit(solution)/shard_map/dot_general | solution.py:520
  222.0 0.0 copy-done.16
  222.0 0.0 copy-done.18
  222.1 0.0 copy-start.5
  222.1 0.0 copy-start.12
  222.1 2.9 %fusion.12 = bf16[1,768,2048]{2,1,0:T(8,128)(2,1)} fusion(f32[256]{0:T(256)S(1)} %bitcast.69, bf16[2,256,2048]{2,1,0:T(8,128)(2,1)S(1)} %copy-done.3, f32[256,768]{1,0:T(8,128)S(1)} %copy-done.18, f32[256,768]{1,0:T(8,128)S(1)} %copy-done.16), kind=kOutput, calls=%fused_computation.16 | convolution fusion | flops 809631744 | bytes 5768192 | tf_op jit(solution)/shard_map/dot_general | solution.py:517
  224.9 0.0 copy-done.5
  224.9 1.2 copy-done.12
  226.1 3.3 %convolution_convert_fusion.4 = bf16[1024,512]{1,0:T(8,128)(2,1)} fusion(bf16[1024,2048]{1,0:T(8,128)(2,1)S(1)} %copy-done.5, bf16[512,2048]{1,0:T(8,128)(2,1)S(1)} %copy-done.12), kind=kOutput, calls=%fused_computation.26 | convolution fusion | flops 2148007936 | bytes 7340032 | tf_op jit(solution)/shard_map/dot_general | solution.py:575
  229.4 15.0 %reduce-scatter.2.cloned.1.call-done = bf16[512,512]{0,1:T(8,128)(2,1)} async-done(((bf16[512,2048]{0,1:T(8,128)(2,1)}), bf16[512,512]{0,1:T(8,128)(2,1)}) %reduce-scatter.2.cloned.1.call-update) | async-done | bytes 524304 | tf_op jit(solution)/shard_map/reduce_scatter | solution.py:581
  244.4 2.0 copy.16
  (8 shorter events, 0.1 us)
Async XLA Ops:
  7.2 100.5 %copy-start = (bf16[1,2048,768]{2,1,0:T(8,128)(2,1)S(1)}, bf16[1,2048,768]{2,1,0:T(8,128)(2,1)}, u32[]{:S(2)}) copy-start(bf16[1,2048,768]{2,1,0:T(8,128)(2,1)} %param.14) | copy-start | bytes 9437188
  7.2 237.2 %reduce-scatter.2.cloned.1.call-start = ((), (), s32[]{:S(2)}) async-start(), calls=%async_computation.1 | async-start | bytes 2621440 | tf_op jit(solution)/shard_map/reduce_scatter | solution.py:581
  10.4 1.6 copy-start.4
  107.7 3.7 %copy-start.2 = (bf16[2,256,2048]{2,1,0:T(8,128)(2,1)}, bf16[2,256,2048]{2,1,0:T(8,128)(2,1)S(1)}, u32[]{:S(2)}) copy-start(bf16[2,256,2048]{2,1,0:T(8,128)(2,1)S(1)} %shard_map.131) | copy-start | bytes 6291460
  107.7 2.6 %copy-start.6 = (bf16[1,2048,768]{2,1,0:T(8,128)(2,1)S(1)}, bf16[1,2048,768]{2,1,0:T(8,128)(2,1)}, u32[]{:S(2)}) copy-start(bf16[1,2048,768]{2,1,0:T(8,128)(2,1)} %param.15) | copy-start | bytes 9437188
  110.3 3.7 %copy-start.15 = (f32[256,768]{1,0:T(8,128)}, f32[256,768]{1,0:T(8,128)S(1)}, u32[]{:S(2)}) copy-start(f32[256,768]{1,0:T(8,128)S(1)} %fusion.2) | copy-start | bytes 2359300
  110.3 2.5 copy-start.11
  110.3 2.5 copy-start.14
  111.3 2.7 %copy-start.17 = (f32[256,768]{1,0:T(8,128)}, f32[256,768]{1,0:T(8,128)S(1)}, u32[]{:S(2)}) copy-start(f32[256,768]{1,0:T(8,128)S(1)} %fusion.6) | copy-start | bytes 2359300
  114.0 1.0 copy-start.9
  114.1 2.1 copy-start.7
  115.1 1.0 copy-start.1
  116.1 93.1 %copy-start.13 = (bf16[1024,512]{1,0:T(8,128)(2,1)S(1)}, bf16[1024,512]{1,0:T(8,128)(2,1)}, u32[]{:S(2)}) copy-start(bf16[1024,512]{1,0:T(8,128)(2,1)} %param.11) | copy-start | bytes 3145732
  209.2 6.0 %copy-start.8 = (bf16[256,768]{1,0:T(8,128)(2,1)S(1)}, bf16[256,768]{1,0:T(8,128)(2,1)}, u32[]{:S(2)}) copy-start(bf16[256,768]{1,0:T(8,128)(2,1)} %copy-done.7) | copy-start | bytes 1179652
  215.2 4.1 %copy-start.3 = (bf16[2,256,2048]{2,1,0:T(8,128)(2,1)S(1)}, bf16[2,256,2048]{2,1,0:T(8,128)(2,1)}, u32[]{:S(2)}) copy-start(bf16[2,256,2048]{2,1,0:T(8,128)(2,1)} %copy-done.2) | copy-start | bytes 6291460
  215.2 4.1 %copy-start.10 = (bf16[256,768]{1,0:T(8,128)(2,1)S(1)}, bf16[256,768]{1,0:T(8,128)(2,1)}, u32[]{:S(2)}) copy-start(bf16[256,768]{1,0:T(8,128)(2,1)} %copy-done.9) | copy-start | bytes 1179652
  219.3 2.7 %copy-start.16 = (f32[256,768]{1,0:T(8,128)S(1)}, f32[256,768]{1,0:T(8,128)}, u32[]{:S(2)}) copy-start(f32[256,768]{1,0:T(8,128)} %copy-done.15) | copy-start | bytes 2359300
  219.3 2.7 %copy-start.18 = (f32[256,768]{1,0:T(8,128)S(1)}, f32[256,768]{1,0:T(8,128)}, u32[]{:S(2)}) copy-start(f32[256,768]{1,0:T(8,128)} %copy-done.17) | copy-start | bytes 2359300
  222.1 2.9 %copy-start.5 = (bf16[1024,2048]{1,0:T(8,128)(2,1)S(1)}, bf16[1024,2048]{1,0:T(8,128)(2,1)}, u32[]{:S(2)}) copy-start(bf16[1024,2048]{1,0:T(8,128)(2,1)} %shard_map.132) | copy-start | bytes 12582916
  222.1 4.0 %copy-start.12 = (bf16[512,2048]{1,0:T(8,128)(2,1)S(1)}, bf16[512,2048]{1,0:T(8,128)(2,1)}, u32[]{:S(2)}) copy-start(bf16[512,2048]{1,0:T(8,128)(2,1)} %param.17) | copy-start | bytes 6291460
Sparse Core Ops, SparseCore 0:
  215.3 29.0 reduce-scatter.1

commit v3 on v2

--- a/solution.py
+++ b/solution.py
@@ -61,13 +61,13 @@
 
 
 def dispatch_kernel(
-    chunk, x_ref, pick_ref, place_ref, out_ref, gat, stage, recv,
+    chunk, in_ref, grad_ref, pick_ref, place_ref, out_ref, gat, stage, recv,
     up_s, up_r, down_s, down_r, plane_s, plane_r,
 ):
     groups, nz, ny, g, z, y = place()
     planes = groups * ny
     me = g * ny + y
-    rows, width = x_ref.shape[1:]
+    rows, width = in_ref.shape
     slots = stage.shape[1] // planes
     parts = width // chunk
     items = 2 * parts
@@ -79,15 +79,13 @@
         return pl.ds(pl.multiple_of((i % parts) * chunk, chunk), chunk)
 
     def block(i, h):
-        return gat.at[i // parts, pl.ds(pl.multiple_of(h * rows, rows), rows), cols(i)]
+        return gat.at[i, pl.ds(pl.multiple_of(h * rows, rows), rows)]
 
     def up(i, h, s):
-        src = x_ref.at[i // parts, :, cols(i)] if s == 0 else block(i, h)
-        return remote(src, block(i, h), up_s.at[i, s], up_r.at[i, s], above)
+        return remote(block(i, h), block(i, h), up_s.at[i, s], up_r.at[i, s], above)
 
     def down(i, h, s):
-        src = x_ref.at[i // parts, :, cols(i)] if s == 0 else block(i, h)
-        return remote(src, block(i, h), down_s.at[i, s], down_r.at[i, s], below)
+        return remote(block(i, h), block(i, h), down_s.at[i, s], down_r.at[i, s], below)
 
     def own(i):
         @pl.when(z < nz - 1)
@@ -97,9 +95,6 @@
         @pl.when(z > 0)
         def _():
             down(i, z, 0).start()
-
-        here = pl.ds(pl.multiple_of(z * rows, rows), rows)
-        gat[i // parts, here, cols(i)] = x_ref[i // parts, :, cols(i)]
 
     def hops(i):
         for s in range(1, nz):
@@ -126,14 +121,13 @@
         theirs = pl.ds(pl.multiple_of(peer * slots, slots), slots)
         mine = pl.ds(pl.multiple_of(me * slots, slots), slots)
         return remote(
-            stage.at[i // parts, theirs, cols(i)], recv.at[i // parts, mine, cols(i)],
+            stage.at[i, theirs], recv.at[i, mine],
             plane_s.at[i, k - 1], plane_r.at[i, k - 1], at_plane(peer, z, ny),
         )
 
     def pick(i):
-        a = i // parts
-        stage[a, :, cols(i)] = jnp.dot(
-            pick_ref[...], gat[a, :, cols(i)], preferred_element_type=jnp.float32
+        stage[i] = jnp.dot(
+            pick_ref[...], gat[i], preferred_element_type=jnp.float32
         ).astype(jnp.bfloat16)
 
         def one(k, carry):
@@ -142,7 +136,7 @@
 
         lax.fori_loop(1, planes, one, 0)
         mine = pl.ds(pl.multiple_of(me * slots, slots), slots)
-        recv[a, mine, cols(i)] = stage[a, mine, cols(i)]
+        recv[i, mine] = stage[i, mine]
 
     def finish(i):
         a = i // parts
@@ -153,8 +147,13 @@
 
         lax.fori_loop(1, planes, one, 0)
         out_ref[a, :, cols(i)] = jnp.dot(
-            place_ref[...], recv[a, :, cols(i)], preferred_element_type=jnp.float32
+            place_ref[...], recv[i], preferred_element_type=jnp.float32
         ).astype(jnp.bfloat16)
+
+    here = pl.ds(pl.multiple_of(z * rows, rows), rows)
+    for i in range(items):
+        ref = in_ref if i < parts else grad_ref
+        gat[i, here] = ref[:, (i % parts) * chunk : (i % parts + 1) * chunk]
 
     own(0)
     own(1)
@@ -195,23 +194,23 @@
     lax.fori_loop(0, items, drain, 0)
 
 
-def dispatch(x, picker, placer, nz, planes):
-    _, rows, width = x.shape
+def dispatch(moe_input, out_grad, picker, placer, nz, planes):
+    rows, width = moe_input.shape
     taken = placer.shape[1]
     cap = placer.shape[0]
-    chunk = width // 8
+    chunk = width // 4
     items = 2 * (width // chunk)
     dma = pltpu.SemaphoreType.DMA
     vmem = pl.BlockSpec(memory_space=pltpu.VMEM)
     return pl.pallas_call(
         functools.partial(dispatch_kernel, chunk),
         out_shape=jax.ShapeDtypeStruct((2, cap, width), jnp.bfloat16),
-        in_specs=[vmem] * 3,
+        in_specs=[vmem] * 4,
         out_specs=vmem,
         scratch_shapes=[
-            pltpu.VMEM((2, nz * rows, width), jnp.bfloat16),
-            pltpu.VMEM((2, taken, width), jnp.bfloat16),
-            pltpu.VMEM((2, taken, width), jnp.bfloat16),
+            pltpu.VMEM((items, nz * rows, chunk), jnp.bfloat16),
+            pltpu.VMEM((items, taken, chunk), jnp.bfloat16),
+            pltpu.VMEM((items, taken, chunk), jnp.bfloat16),
             dma((items, nz - 1)), dma((items, nz - 1)),
             dma((items, nz - 1)), dma((items, nz - 1)),
             dma((items, planes - 1)), dma((items, planes - 1)),
@@ -219,26 +218,30 @@
         compiler_params=pltpu.CompilerParams(
             collective_id=0, has_side_effects=True, vmem_limit_bytes=48 * 2**20
         ),
-    )(x, picker, placer)
+    )(moe_input, out_grad, picker, placer)
 
 
 def collect_kernel(
-    chunk, rg_ref, place_ref, pick_ref, og_ref, piece, stage, recv, part,
-    from_down, from_up, to_down, to_up,
-    plane_s, plane_r, rd_s, rd_r, ru_s, ru_r, up_s, up_r, down_s, down_r, y_s, y_r,
+    rg_ref, place_ref, pick_ref, og_ref, context_ref, wout_ref, ctx_ref, proj_ref,
+    stage, recv, part, piece, ctx, proj, proj_in, from_down, from_up, to_down, to_up,
+    plane_s, plane_r, rd_s, rd_r, ru_s, ru_r, up_s, up_r, down_s, down_r, y_s, y_r, proj_s, proj_r,
 ):
     groups, nz, ny, g, z, y = place()
     planes = groups * ny
     me = g * ny + y
     rows, width = og_ref.shape
-    slots = stage.shape[0] // planes
-    parts = width // chunk
+    slots = stage.shape[1] // planes
+    parts = groups
+    chunk = width // parts
     above = (g, (z + 1) * ny + y)
     below = (g, (z - 1) * ny + y)
     greet(g, z, y, nz, ny, planes)
 
-    def cols(q):
-        return pl.ds(pl.multiple_of(q * chunk, chunk), chunk)
+    def owner(q, group):
+        return lax.rem(group + q + 1, groups)
+
+    def cols(q, group=g):
+        return pl.ds(pl.multiple_of(owner(q, group) * chunk, chunk), chunk)
 
     def line(h):
         return pl.ds(pl.multiple_of(h * rows, rows), rows)
@@ -248,24 +251,24 @@
         theirs = pl.ds(pl.multiple_of(peer * slots, slots), slots)
         mine = pl.ds(pl.multiple_of(me * slots, slots), slots)
         return remote(
-            stage.at[theirs, cols(q)], recv.at[mine, cols(q)],
+            stage.at[q, theirs], recv.at[q, mine],
             plane_s.at[q, k - 1], plane_r.at[q, k - 1], at_plane(peer, z, ny),
         )
 
     def reduce_down(q, h):
         return remote(
-            to_down.at[line(h), cols(q)], from_up.at[line(h), cols(q)],
+            to_down.at[q, line(h)], from_up.at[q, line(h)],
             rd_s.at[q, h], rd_r.at[q, h], below,
         )
 
     def reduce_up(q, h):
         return remote(
-            to_up.at[line(h), cols(q)], from_down.at[line(h), cols(q)],
+            to_up.at[q, line(h)], from_down.at[q, line(h)],
             ru_s.at[q, h], ru_r.at[q, h], above,
         )
 
     def block(q, h, side):
-        return piece.at[pl.ds(pl.multiple_of((h * ny + side) * rows, rows), rows), cols(q)]
+        return piece.at[q, pl.ds(pl.multiple_of((h * ny + side) * rows, rows), rows)]
 
     def up(q, h, s, k=0):
         this = block(q, h, lax.rem(y + k, ny))
@@ -331,9 +334,13 @@
             sideways(q, h, k).start()
 
     def scatter(q):
-        stage[:, cols(q)] = jnp.dot(
-            place_ref[...], rg_ref[:, cols(q)], preferred_element_type=jnp.float32
-        ).astype(jnp.bfloat16)
+        span = ny * slots
+        for group in range(groups):
+            stage[q, group * span : (group + 1) * span] = jnp.dot(
+                place_ref[group * span : (group + 1) * span, :],
+                rg_ref[:, cols(q, group)],
+                preferred_element_type=jnp.float32,
+            ).astype(jnp.bfloat16)
 
         def one(k, carry):
             plane(q, k).start()
@@ -341,7 +348,7 @@
 
         lax.fori_loop(1, planes, one, 0)
         mine = pl.ds(pl.multiple_of(me * slots, slots), slots)
-        recv[mine, cols(q)] = stage[mine, cols(q)]
+        recv[q, mine] = stage[q, mine]
 
     def gathered(q):
         def one(k, carry):
@@ -349,29 +356,29 @@
             return carry
 
         lax.fori_loop(1, planes, one, 0)
-        part[:, cols(q)] = jnp.dot(
-            pick_ref[...], recv[:, cols(q)], preferred_element_type=jnp.float32
+        part[q] = jnp.dot(
+            pick_ref[...], recv[q], preferred_element_type=jnp.float32
         )
 
     def hop(q, h):
         @pl.when(z == nz - 1 - h)
         def _():
             for far in range(nz - 1 - h):
-                total = part[line(far), cols(q)]
+                total = part[q, line(far)]
                 if h > 0:
                     reduce_down(q, far).wait_recv()
-                    total = total + from_up[line(far), cols(q)].astype(jnp.float32)
-                to_down[line(far), cols(q)] = total.astype(jnp.bfloat16)
+                    total = total + from_up[q, line(far)].astype(jnp.float32)
+                to_down[q, line(far)] = total.astype(jnp.bfloat16)
                 reduce_down(q, far).start()
 
         @pl.when(z == h)
         def _():
             for far in range(nz - 1, h, -1):
-                total = part[line(far), cols(q)]
+                total = part[q, line(far)]
                 if h > 0:
                     reduce_up(q, far).wait_recv()
-                    total = total + from_down[line(far), cols(q)].astype(jnp.float32)
-                to_up[line(far), cols(q)] = total.astype(jnp.bfloat16)
+                    total = total + from_down[q, line(far)].astype(jnp.float32)
+                to_up[q, line(far)] = total.astype(jnp.bfloat16)
                 reduce_up(q, far).start()
 
     def total(q):
@@ -380,16 +387,16 @@
         @pl.when(z < nz - 1)
         def _():
             reduce_down(q, z).wait_recv()
-            part[here, cols(q)] += from_up[here, cols(q)].astype(jnp.float32)
+            part[q, here] += from_up[q, here].astype(jnp.float32)
 
         @pl.when(z > 0)
         def _():
             reduce_up(q, z).wait_recv()
-            part[here, cols(q)] += from_down[here, cols(q)].astype(jnp.float32)
+            part[q, here] += from_down[q, here].astype(jnp.float32)
 
         mine = pl.ds(pl.multiple_of((z * ny + y) * rows, rows), rows)
-        piece[mine, cols(q)] = (
-            og_ref[:, cols(q)].astype(jnp.float32) + part[here, cols(q)]
+        piece[q, mine] = (
+            og_ref[:, cols(q)].astype(jnp.float32) + part[q, here]
         ).astype(jnp.bfloat16)
 
         leave(q, 0)
@@ -408,20 +415,69 @@
                 else:
                     along(q, s - 1, k)
 
+    def project(q):
+        @pl.when(jnp.logical_not(sideways_first(q)))
+        def _():
+            for h in range(nz):
+                for k in range(1, ny):
+                    beside(q, h, k).wait_recv()
+
+        totals = piece[q]
+        term = lax.dot_general(
+            totals, wout_ref[:, cols(q)], (((1,), (1,)), ((), ())),
+            preferred_element_type=jnp.float32,
+        )
+
+        @pl.when(q == 0)
+        def _():
+            ctx[...] = term
+
+        @pl.when(q > 0)
+        def _():
+            ctx[...] += term
+
+        share_of = lax.dot_general(
+            context_ref[...], totals, (((0,), (0,)), ((), ())),
+            preferred_element_type=jnp.float32,
+        )
+
+        @pl.when(q < parts - 1)
+        def _():
+            proj[q] = share_of.astype(jnp.bfloat16)
+            to_owner(q).start()
+
+        @pl.when(q == parts - 1)
+        def _():
+            acc = share_of
+            for other in range(parts - 1):
+                to_owner(other).wait_recv()
+                acc = acc + proj_in[other].astype(jnp.float32)
+            proj_ref[...] = acc.astype(jnp.bfloat16)
+            ctx_ref[...] = ctx[...].astype(jnp.bfloat16)
+
+    def to_owner(q):
+        return remote(
+            proj.at[q], proj_in.at[q], proj_s.at[q], proj_r.at[q],
+            (owner(q, g), z * ny + y),
+        )
+
     stages = [scatter, gathered]
     stages += [functools.partial(lambda h, q: hop(q, h), h) for h in range(nz - 1)]
     stages += [total]
     stages += [functools.partial(lambda s, q: forward(q, s), s) for s in range(1, nz + 1)]
+    stages += [project]
+
+    last = len(stages) - 1
 
     def step(t, carry):
-        for k in reversed(range(len(stages))):
+        for k in [*reversed(range(last)), last]:
             @pl.when((t >= k) & (t - k < parts))
             def _():
                 stages[k](t - k)
 
         return carry
 
-    lax.fori_loop(0, parts + len(stages) - 1, step, 0)
+    lax.fori_loop(0, parts + last, step, 0)
 
     def drain(q, carry):
         def one(k, c):
@@ -443,10 +499,6 @@
                 @pl.when(shared)
                 def _():
                     sideways(q, h, k).wait_send()
-
-                @pl.when(jnp.logical_not(sideways_first(q)))
-                def _():
-                    beside(q, h, k).wait_recv()
         for s in range(nz - 1):
             for k in range(ny):
                 used = sideways_first(q) if k else (z >= 0)
@@ -459,28 +511,42 @@
                 def _():
                     down(q, z + s, s, k).wait_send()
 
+        @pl.when(q < parts - 1)
+        def _():
+            to_owner(q).wait_send()
+
         return carry
 
     lax.fori_loop(0, parts, drain, 0)
 
 
-def collect(row_grad, placer, picker, out_grad, nz, ny, planes):
+def collect(row_grad, placer, picker, out_grad, context, w_out, groups, nz, ny):
     rows, width = out_grad.shape
+    features = w_out.shape[0]
     taken = placer.shape[0]
-    chunk = width // 8
-    parts = width // chunk
+    planes = groups * ny
+    parts = groups
+    chunk = width // parts
+    tokens = nz * ny * rows
     dma = pltpu.SemaphoreType.DMA
     vmem = pl.BlockSpec(memory_space=pltpu.VMEM)
-    line = (nz * rows, width)
+    line = (parts, nz * rows, chunk)
     return pl.pallas_call(
-        functools.partial(collect_kernel, chunk),
-        out_shape=jax.ShapeDtypeStruct((nz * ny * rows, width), jnp.bfloat16),
-        in_specs=[vmem] * 4,
-        out_specs=vmem,
+        collect_kernel,
+        out_shape=(
+            jax.ShapeDtypeStruct((tokens, features), jnp.bfloat16),
+            jax.ShapeDtypeStruct((features, chunk), jnp.bfloat16),
+        ),
+        in_specs=[vmem] * 6,
+        out_specs=(vmem, vmem),
         scratch_shapes=[
-            pltpu.VMEM((taken, width), jnp.bfloat16),
-            pltpu.VMEM((taken, width), jnp.bfloat16),
+            pltpu.VMEM((parts, taken, chunk), jnp.bfloat16),
+            pltpu.VMEM((parts, taken, chunk), jnp.bfloat16),
             pltpu.VMEM(line, jnp.float32),
+            pltpu.VMEM((parts, tokens, chunk), jnp.bfloat16),
+            pltpu.VMEM((tokens, features), jnp.float32),
+            pltpu.VMEM((parts - 1, features, chunk), jnp.bfloat16),
+            pltpu.VMEM((parts - 1, features, chunk), jnp.bfloat16),
             pltpu.VMEM(line, jnp.bfloat16),
             pltpu.VMEM(line, jnp.bfloat16),
             pltpu.VMEM(line, jnp.bfloat16),
@@ -491,11 +557,12 @@
             dma((parts, ny, nz - 1)), dma((parts, ny, nz - 1)),
             dma((parts, ny, nz - 1)), dma((parts, ny, nz - 1)),
             dma((parts, nz, ny - 1)), dma((parts, nz, ny - 1)),
+            dma((parts - 1,)), dma((parts - 1,)),
         ],
         compiler_params=pltpu.CompilerParams(
-            collective_id=1, has_side_effects=True, vmem_limit_bytes=48 * 2**20
+            collective_id=1, has_side_effects=True, vmem_limit_bytes=50 * 2**20
         ),
-    )(row_grad, placer, picker, out_grad)
+    )(row_grad, placer, picker, out_grad, context, w_out)
 
 
 def expert_backward(rows_in, rows_grad, scales, gate_w, up_w, down_w):
@@ -567,26 +634,19 @@
     capacity = selected.shape[1]
     most = max(4, (2 * capacity + devices - 1) // devices)
     picker, placer = tables(selected, tok_rows, most)
-    rows = dispatch(jnp.stack([moe_input, out_grad]), picker, placer, nz, planes)
+    rows = dispatch(moe_input, out_grad, picker, placer, nz, planes)
     grad_gate, grad_up, grad_down, row_grad = expert_backward(
         rows[0], rows[1], gate_scale[0], w_gate[0], w_up[0], w_down[0]
     )
-    piece = collect(row_grad, placer.T, picker.T, out_grad, nz, ny, planes)
-    grad_ctx = lax.dot_general(
-        piece, w_out, (((1,), (1,)), ((), ())), preferred_element_type=jnp.float32
-    )
-    grad_proj = lax.dot_general(
-        context, piece, (((0,), (0,)), ((), ())), preferred_element_type=jnp.float32
-    )
-    proj_share = lax.psum_scatter(
-        grad_proj.astype(jnp.bfloat16), "grp", scatter_dimension=1, tiled=True
+    grad_ctx, grad_proj = collect(
+        row_grad, placer.T, picker.T, out_grad, context, w_out, groups, nz, ny
     )
     return (
         grad_gate[None],
         grad_up[None],
         grad_down[None],
-        grad_ctx.astype(jnp.bfloat16),
-        proj_share,
+        grad_ctx,
+        grad_proj,
     )
 
 

time: 254 us -> 221 us (0.87); the launches traced: 253 us -> 218 us
  waiting for transfers between devices: 15 us -> 0 us
  between operations: 14.4 us -> 0.86 us
  matrix products: 24.1 us -> 13.5 us
  Pallas kernels: 189 us -> 195 us
    pallas_call x1, Pallas kernels: 93 us -> 110 us  [collect(): pl.pallas_call(collect_kernel, out_shape=(jax.ShapeDtypeStruct((tokens, f...]
    reduce_scatter x1 -> x0, waiting for transfers between devices: 15 us -> none  [body(): lax.psum_scatter(grad_proj.astype(jnp.bfloat16), 'grp', scatter_dimension...]
    pallas_call x1, Pallas kernels: 95.7 us -> 85.1 us  [dispatch(): pl.pallas_call(functools.partial(dispatch_kernel, chunk), out_shape=jax.S...]
    dot_general x2 -> x0, matrix products: 9.3 us -> none  [the longest x1 5.97 us: body(): lax.dot_general(context, piece, (((0,), (0,)), ((), ())), preferred_eleme...]
    unnamed x40 -> x17, local copies, waits for them, and re-layouts: 6.43 us -> 5.67 us
  transfers between devices with their start and end apart: 1 -> 0, of which waited for: 1 -> 0; matrix products, arithmetic and copies ran while one was open for 5% -> 0% of each run, Pallas kernels for 0% -> 0%
where the time goes in v3:
time: 221 us; the launch traced here: 218 us
  Pallas kernels  195 us (88%)
  matrix products  13.5 us (6%)
  local copies, waits for them, and re-layouts  6.68 us (3%)
    pallas_call x1, Pallas kernels, collect(): pl.pallas_call(collect_kernel, out_shape=(jax.ShapeDtypeStruct((tokens, f...  110 us
    pallas_call x1, Pallas kernels, dispatch(): pl.pallas_call(functools.partial(dispatch_kernel, chunk), out_shape=jax.S...  85.1 us
    unnamed x17, local copies, waits for them, and re-layouts  5.67 us

profile of v3, /device:TPU:0, one launch (start us, length us, event | category | flops | bytes accessed | tf_op | source)
XLA Modules:
  0.0 217.7 jit_solution(7470034565822669968)
XLA Ops:
  0.6 0.0 copy-start
  0.7 0.9 reshape.215
  1.7 0.8 convert_reduce_fusion
  2.6 0.2 select_reduce_fusion
  2.8 0.1 eq.94
  2.9 0.1 fusion.40.place_ref
  3.0 0.1 fusion.39.place_ref
  3.1 0.2 compare_convert_fusion
  3.3 0.0 copy-start.1
  3.3 1.0 copy-done.1
  4.4 0.0 copy-start.3
  4.4 1.0 copy-done.3
  5.4 85.1 %shard_map.131 = bf16[2,256,2048]{2,1,0:T(8,128)(2,1)S(1)} custom-call(bf16[128,2048]{1,0:T(8,128)(2,1)S(1)} %copy-done.3, bf16[128,2048]{1,0:T(8,128)(2,1)S(1)} %copy-done.1, bf16[512,512]{1,0:T(8,128)(2,1)S(1)} %get-tuple-element.16.pick_ref, bf16[256,512]{1,0:T(8,128)(2,1)S(1)} %fusion.39.place_ref), custom_call_target="tpu_custom_call" | custom-call | tf_op jit(solution)/shard_map/pallas_call | solution.py:205
  90.6 0.0 copy-done
  90.6 0.0 copy-start.4
  90.6 1.0 fusion.2
  91.6 0.9 copy-done.4
  92.5 0.0 copy-start.5
  92.5 0.0 copy-start.6
  92.5 1.0 fusion.6
  93.5 0.9 copy-done.5
  94.3 0.0 copy-done.6
  94.3 1.2 multiply_convert_fusion.1
  95.6 2.9 %fusion.12 = bf16[1,768,2048]{2,1,0:T(8,128)(2,1)} fusion(f32[256]{0:T(256)S(1)} %bitcast.59, bf16[2,256,2048]{2,1,0:T(8,128)(2,1)S(1)} %shard_map.131, f32[256,768]{1,0:T(8,128)S(1)} %fusion.6, f32[256,768]{1,0:T(8,128)S(1)} %fusion.2), kind=kOutput, calls=%fused_computation.15 | convolution fusion | flops 809631744 | bytes 5768192 | tf_op jit(solution)/shard_map/dot_general | solution.py:584
  98.5 1.0 fusion
  99.5 0.0 copy-start.2
  99.5 1.0 fusion.16.rg_ref
  100.5 0.0 copy-done.2
  100.5 109.9 %shard_map.132 = (bf16[1024,512]{1,0:T(8,128)(2,1)S(1)}, bf16[512,512]{1,0:T(8,128)(2,1)S(1)}) custom-call(bf16[256,2048]{1,0:T(8,128)(2,1)S(1)} %fusion.16.rg_ref, bf16[512,256]{1,0:T(8,128)(2,1)S(1)} %fusion.40.place_ref, bf16[512,512]{1,0:T(8,128)(2,1)S(1)} %get-tuple-element.15.pick_ref, bf16[128,2048]{1,0:T(8,128)(2,1)S(1)} %copy-done.2, ...), custom_call_target="tpu_custom_call" | custom-call | tf_op jit(solution)/shard_map/pallas_call | solution.py:534
  210.5 2.7 %fusion.11 = bf16[1,2048,768]{2,1,0:T(8,128)(2,1)} fusion(bf16[256,768]{1,0:T(8,128)(2,1)S(1)} %get-tuple-element.11, bf16[2,256,2048]{2,1,0:T(8,128)(2,1)S(1)} %shard_map.131), kind=kOutput, calls=%fused_computation.14 | convolution fusion | flops 806879232 | bytes 4587520 | tf_op jit(solution)/shard_map/dot_general | solution.py:590
  213.2 2.7 %fusion.10 = bf16[1,2048,768]{2,1,0:T(8,128)(2,1)} fusion(bf16[256,768]{1,0:T(8,128)(2,1)S(1)} %get-tuple-element.12, bf16[2,256,2048]{2,1,0:T(8,128)(2,1)S(1)} %shard_map.131), kind=kOutput, calls=%fused_computation.13 | convolution fusion | flops 806879232 | bytes 4587520 | tf_op jit(solution)/shard_map/dot_general | solution.py:587
  215.9 1.0 copy.18
  216.9 0.8 copy.19
  (8 shorter events, 0.1 us)
Async XLA Ops:
  0.6 89.9 %copy-start = (bf16[1,2048,768]{2,1,0:T(8,128)(2,1)S(1)}, bf16[1,2048,768]{2,1,0:T(8,128)(2,1)}, u32[]{:S(2)}) copy-start(bf16[1,2048,768]{2,1,0:T(8,128)(2,1)} %param.14) | copy-start | bytes 9437188
  3.3 1.0 copy-start.1
  4.4 1.0 copy-start.3
  90.6 1.9 copy-start.4
  92.5 1.9 copy-start.5
  92.5 1.9 copy-start.6
  99.5 1.1 copy-start.2

commit v4 on v3

--- a/solution.py
+++ b/solution.py
@@ -36,13 +36,9 @@
     me = g * ny + y
     barrier = pltpu.get_barrier_semaphore()
 
-    @pl.when(z > 0)
-    def _():
-        pl.semaphore_signal(barrier, inc=1, device_id=(g, (z - 1) * ny + y), device_id_type=MESH)
-
-    @pl.when(z < nz - 1)
-    def _():
-        pl.semaphore_signal(barrier, inc=1, device_id=(g, (z + 1) * ny + y), device_id_type=MESH)
+    for k in range(1, nz):
+        height = lax.rem(z + k, nz)
+        pl.semaphore_signal(barrier, inc=1, device_id=(g, height * ny + y), device_id_type=MESH)
 
     def one(k, carry):
         peer = lax.rem(me + k, planes)
@@ -50,8 +46,7 @@
         return carry
 
     lax.fori_loop(1, planes, one, 0)
-    beside = jnp.where(z > 0, 1, 0) + jnp.where(z < nz - 1, 1, 0)
-    pl.semaphore_wait(barrier, planes - 1 + beside)
+    pl.semaphore_wait(barrier, planes - 1 + nz - 1)
 
 
 def remote(src, dst, send, recv, device):
@@ -62,7 +57,7 @@
 
 def dispatch_kernel(
     chunk, in_ref, grad_ref, pick_ref, place_ref, out_ref, gat, stage, recv,
-    up_s, up_r, down_s, down_r, plane_s, plane_r,
+    up_s, up_r, down_s, down_r, plane_s, plane_r, own_s,
 ):
     groups, nz, ny, g, z, y = place()
     planes = groups * ny
@@ -71,8 +66,18 @@
     slots = stage.shape[1] // planes
     parts = width // chunk
     items = 2 * parts
+    ahead = 3
     above = (g, (z + 1) * ny + y)
     below = (g, (z - 1) * ny + y)
+    here = pl.ds(pl.multiple_of(z * rows, rows), rows)
+
+    def fetch(i):
+        ref = in_ref if i < parts else grad_ref
+        taken = ref.at[:, pl.ds((i % parts) * chunk, chunk)]
+        return pltpu.make_async_copy(taken, gat.at[i, here], own_s.at[i])
+
+    for i in range(items):
+        fetch(i).start()
     greet(g, z, y, nz, ny, planes)
 
     def cols(i):
@@ -150,29 +155,28 @@
             place_ref[...], recv[i], preferred_element_type=jnp.float32
         ).astype(jnp.bfloat16)
 
-    here = pl.ds(pl.multiple_of(z * rows, rows), rows)
     for i in range(items):
-        ref = in_ref if i < parts else grad_ref
-        gat[i, here] = ref[:, (i % parts) * chunk : (i % parts + 1) * chunk]
-
-    own(0)
-    own(1)
+        fetch(i).wait()
+
+    for i in range(ahead):
+        own(i)
 
     def step(i, carry):
-        @pl.when(i + 2 < items)
-        def _():
-            own(i + 2)
+        @pl.when(i + ahead < items)
+        def _():
+            own(i + ahead)
 
         hops(i)
         pick(i)
 
-        @pl.when(i > 0)
-        def _():
-            finish(i - 1)
+        @pl.when(i > 1)
+        def _():
+            finish(i - 2)
 
         return carry
 
     lax.fori_loop(0, items, step, 0)
+    finish(items - 2)
     finish(items - 1)
 
     def drain(i, carry):
@@ -205,7 +209,7 @@
     return pl.pallas_call(
         functools.partial(dispatch_kernel, chunk),
         out_shape=jax.ShapeDtypeStruct((2, cap, width), jnp.bfloat16),
-        in_specs=[vmem] * 4,
+        in_specs=[pl.BlockSpec(memory_space=pl.ANY)] * 2 + [vmem] * 2,
         out_specs=vmem,
         scratch_shapes=[
             pltpu.VMEM((items, nz * rows, chunk), jnp.bfloat16),
@@ -214,17 +218,18 @@
             dma((items, nz - 1)), dma((items, nz - 1)),
             dma((items, nz - 1)), dma((items, nz - 1)),
             dma((items, planes - 1)), dma((items, planes - 1)),
+            dma((items,)),
         ],
         compiler_params=pltpu.CompilerParams(
-            collective_id=0, has_side_effects=True, vmem_limit_bytes=48 * 2**20
+            collective_id=0, has_side_effects=True, vmem_limit_bytes=24 * 2**20
         ),
     )(moe_input, out_grad, picker, placer)
 
 
 def collect_kernel(
     rg_ref, place_ref, pick_ref, og_ref, context_ref, wout_ref, ctx_ref, proj_ref,
-    stage, recv, part, piece, ctx, proj, proj_in, from_down, from_up, to_down, to_up,
-    plane_s, plane_r, rd_s, rd_r, ru_s, ru_r, up_s, up_r, down_s, down_r, y_s, y_r, proj_s, proj_r,
+    stage, recv, part, piece, ctx, proj, proj_in, to_line, from_line,
+    plane_s, plane_r, sum_s, sum_r, up_s, up_r, down_s, down_r, y_s, y_r, proj_s, proj_r,
 ):
     groups, nz, ny, g, z, y = place()
     planes = groups * ny
@@ -255,31 +260,28 @@
             plane_s.at[q, k - 1], plane_r.at[q, k - 1], at_plane(peer, z, ny),
         )
 
-    def reduce_down(q, h):
+    def to_height(q, k):
+        h = lax.rem(z + k, nz)
         return remote(
-            to_down.at[q, line(h)], from_up.at[q, line(h)],
-            rd_s.at[q, h], rd_r.at[q, h], below,
-        )
-
-    def reduce_up(q, h):
+            to_line.at[q, line(h)], from_line.at[q, line(z)],
+            sum_s.at[q, k - 1], sum_r.at[q, k - 1], (g, h * ny + y),
+        )
+
+    def from_height(q, k):
+        h = lax.rem(z + k, nz)
         return remote(
-            to_up.at[q, line(h)], from_down.at[q, line(h)],
-            ru_s.at[q, h], ru_r.at[q, h], above,
+            to_line.at[q, line(h)], from_line.at[q, line(h)],
+            sum_s.at[q, nz - 1 - k], sum_r.at[q, nz - 1 - k], (g, h * ny + y),
         )
 
     def block(q, h, side):
         return piece.at[q, pl.ds(pl.multiple_of((h * ny + side) * rows, rows), rows)]
 
-    def up(q, h, s, k=0):
-        this = block(q, h, lax.rem(y + k, ny))
-        return remote(this, this, up_s.at[q, k, s], up_r.at[q, k, s], above)
-
-    def down(q, h, s, k=0):
-        this = block(q, h, lax.rem(y + k, ny))
-        return remote(this, this, down_s.at[q, k, s], down_r.at[q, k, s], below)
-
-    def sideways_first(q):
-        return q % 4 == 1
+    def up(q, h, s):
+        return remote(block(q, h, y), block(q, h, y), up_s.at[q, s], up_r.at[q, s], above)
+
+    def down(q, h, s):
+        return remote(block(q, h, y), block(q, h, y), down_s.at[q, s], down_r.at[q, s], below)
 
     def beside(q, h, k):
         side = lax.rem(y + k, ny)
@@ -287,40 +289,6 @@
             block(q, h, y), block(q, h, side), y_s.at[q, h, ny - 1 - k],
             y_r.at[q, h, ny - 1 - k], (g, z * ny + side),
         )
-
-    def leave(q, k):
-        @pl.when(z < nz - 1)
-        def _():
-            up(q, z, 0, k).start()
-
-        @pl.when(z > 0)
-        def _():
-            down(q, z, 0, k).start()
-
-    def along(q, s, k):
-        @pl.when(z - s >= 0)
-        def _():
-            up(q, z - s, s - 1, k).wait_recv()
-            if s < nz - 1:
-                @pl.when(z < nz - 1)
-                def _():
-                    up(q, z - s, s, k).start()
-            if k == 0:
-                @pl.when(jnp.logical_not(sideways_first(q)))
-                def _():
-                    share(q, z - s)
-
-        @pl.when(z + s < nz)
-        def _():
-            down(q, z + s, s - 1, k).wait_recv()
-            if s < nz - 1:
-                @pl.when(z > 0)
-                def _():
-                    down(q, z + s, s, k).start()
-            if k == 0:
-                @pl.when(jnp.logical_not(sideways_first(q)))
-                def _():
-                    share(q, z + s)
 
     def sideways(q, h, k):
         side = lax.rem(y + k, ny)
@@ -356,71 +324,55 @@
             return carry
 
         lax.fori_loop(1, planes, one, 0)
-        part[q] = jnp.dot(
-            pick_ref[...], recv[q], preferred_element_type=jnp.float32
-        )
-
-    def hop(q, h):
-        @pl.when(z == nz - 1 - h)
-        def _():
-            for far in range(nz - 1 - h):
-                total = part[q, line(far)]
-                if h > 0:
-                    reduce_down(q, far).wait_recv()
-                    total = total + from_up[q, line(far)].astype(jnp.float32)
-                to_down[q, line(far)] = total.astype(jnp.bfloat16)
-                reduce_down(q, far).start()
-
-        @pl.when(z == h)
-        def _():
-            for far in range(nz - 1, h, -1):
-                total = part[q, line(far)]
-                if h > 0:
-                    reduce_up(q, far).wait_recv()
-                    total = total + from_down[q, line(far)].astype(jnp.float32)
-                to_up[q, line(far)] = total.astype(jnp.bfloat16)
-                reduce_up(q, far).start()
+        sums = jnp.dot(pick_ref[...], recv[q], preferred_element_type=jnp.float32)
+        part[q] = sums
+        to_line[q] = sums.astype(jnp.bfloat16)
+        for k in range(1, nz):
+            to_height(q, k).start()
 
     def total(q):
         here = line(z)
+        acc = part[q, here]
+        for k in range(1, nz):
+            from_height(q, k).wait_recv()
+            h = lax.rem(z + k, nz)
+            acc = acc + from_line[q, line(h)].astype(jnp.float32)
+        mine = pl.ds(pl.multiple_of((z * ny + y) * rows, rows), rows)
+        piece[q, mine] = (og_ref[:, cols(q)].astype(jnp.float32) + acc).astype(jnp.bfloat16)
 
         @pl.when(z < nz - 1)
         def _():
-            reduce_down(q, z).wait_recv()
-            part[q, here] += from_up[q, here].astype(jnp.float32)
+            up(q, z, 0).start()
 
         @pl.when(z > 0)
         def _():
-            reduce_up(q, z).wait_recv()
-            part[q, here] += from_down[q, here].astype(jnp.float32)
-
-        mine = pl.ds(pl.multiple_of((z * ny + y) * rows, rows), rows)
-        piece[q, mine] = (
-            og_ref[:, cols(q)].astype(jnp.float32) + part[q, here]
-        ).astype(jnp.bfloat16)
-
-        leave(q, 0)
+            down(q, z, 0).start()
+
         share(q, z)
 
     def forward(q, s):
-        if s < nz:
-            along(q, s, 0)
-
-        @pl.when(sideways_first(q))
-        def _():
+        @pl.when(z - s >= 0)
+        def _():
+            up(q, z - s, s - 1).wait_recv()
+            if s < nz - 1:
+                @pl.when(z < nz - 1)
+                def _():
+                    up(q, z - s, s).start()
+            share(q, z - s)
+
+        @pl.when(z + s < nz)
+        def _():
+            down(q, z + s, s - 1).wait_recv()
+            if s < nz - 1:
+                @pl.when(z > 0)
+                def _():
+                    down(q, z + s, s).start()
+            share(q, z + s)
+
+    def project(q):
+        for h in range(nz):
             for k in range(1, ny):
-                if s == 1:
-                    beside(q, z, k).wait_recv()
-                    leave(q, k)
-                else:
-                    along(q, s - 1, k)
-
-    def project(q):
-        @pl.when(jnp.logical_not(sideways_first(q)))
-        def _():
-            for h in range(nz):
-                for k in range(1, ny):
-                    beside(q, h, k).wait_recv()
+                beside(q, h, k).wait_recv()
 
         totals = piece[q]
         term = lax.dot_general(
@@ -437,7 +389,7 @@
             ctx[...] += term
 
         share_of = lax.dot_general(
-            context_ref[...], totals, (((0,), (0,)), ((), ())),
+            context_ref[...], totals, (((1,), (0,)), ((), ())),
             preferred_element_type=jnp.float32,
         )
 
@@ -461,10 +413,8 @@
             (owner(q, g), z * ny + y),
         )
 
-    stages = [scatter, gathered]
-    stages += [functools.partial(lambda h, q: hop(q, h), h) for h in range(nz - 1)]
-    stages += [total]
-    stages += [functools.partial(lambda s, q: forward(q, s), s) for s in range(1, nz + 1)]
+    stages = [scatter, gathered, total]
+    stages += [functools.partial(lambda s, q: forward(q, s), s) for s in range(1, nz)]
     stages += [project]
 
     last = len(stages) - 1
@@ -485,31 +435,19 @@
             return c
 
         lax.fori_loop(1, planes, one, 0)
+        for k in range(1, nz):
+            to_height(q, k).wait_send()
         for h in range(nz):
-            @pl.when(h < z)
+            for k in range(1, ny):
+                sideways(q, h, k).wait_send()
+        for s in range(nz - 1):
+            @pl.when((z - s >= 0) & (z < nz - 1))
             def _():
-                reduce_down(q, h).wait_send()
-
-            @pl.when(h > z)
+                up(q, z - s, s).wait_send()
+
+            @pl.when((z + s < nz) & (z > 0))
             def _():
-                reduce_up(q, h).wait_send()
-
-            shared = jnp.logical_or(h == z, jnp.logical_not(sideways_first(q)))
-            for k in range(1, ny):
-                @pl.when(shared)
-                def _():
-                    sideways(q, h, k).wait_send()
-        for s in range(nz - 1):
-            for k in range(ny):
-                used = sideways_first(q) if k else (z >= 0)
-
-                @pl.when(used & (z - s >= 0) & (z < nz - 1))
-                def _():
-                    up(q, z - s, s, k).wait_send()
-
-                @pl.when(used & (z + s < nz) & (z > 0))
-                def _():
-                    down(q, z + s, s, k).wait_send()
+                down(q, z + s, s).wait_send()
 
         @pl.when(q < parts - 1)
         def _():
@@ -549,18 +487,15 @@
             pltpu.VMEM((parts - 1, features, chunk), jnp.bfloat16),
             pltpu.VMEM(line, jnp.bfloat16),
             pltpu.VMEM(line, jnp.bfloat16),
-            pltpu.VMEM(line, jnp.bfloat16),
-            pltpu.VMEM(line, jnp.bfloat16),
             dma((parts, planes - 1)), dma((parts, planes - 1)),
-            dma((parts, nz)), dma((parts, nz)),
-            dma((parts, nz)), dma((parts, nz)),
-            dma((parts, ny, nz - 1)), dma((parts, ny, nz - 1)),
-            dma((parts, ny, nz - 1)), dma((parts, ny, nz - 1)),
+            dma((parts, nz - 1)), dma((parts, nz - 1)),
+            dma((parts, nz - 1)), dma((parts, nz - 1)),
+            dma((parts, nz - 1)), dma((parts, nz - 1)),
             dma((parts, nz, ny - 1)), dma((parts, nz, ny - 1)),
             dma((parts - 1,)), dma((parts - 1,)),
         ],
         compiler_params=pltpu.CompilerParams(
-            collective_id=1, has_side_effects=True, vmem_limit_bytes=50 * 2**20
+            collective_id=1, has_side_effects=True, vmem_limit_bytes=40 * 2**20
         ),
     )(row_grad, placer, picker, out_grad, context, w_out)
 
@@ -639,7 +574,7 @@
         rows[0], rows[1], gate_scale[0], w_gate[0], w_up[0], w_down[0]
     )
     grad_ctx, grad_proj = collect(
-        row_grad, placer.T, picker.T, out_grad, context, w_out, groups, nz, ny
+        row_grad, placer.T, picker.T, out_grad, context.T, w_out, groups, nz, ny
     )
     return (
         grad_gate[None],

time: 221 us -> 218 us (0.986)
  Pallas kernels: 195 us -> 185 us
  local copies, waits for them, and re-layouts: 6.68 us -> 12 us
    pallas_call x1, Pallas kernels: 110 us -> 100 us  [collect(): pl.pallas_call(collect_kernel, out_shape=(jax.ShapeDtypeStruct((tokens, f...]
    unnamed x17 -> x28, local copies, waits for them, and re-layouts: 5.67 us -> 11 us
where the time goes in v4:
time: 218 us; the launch traced here: 215 us
  Pallas kernels  185 us (85%)
  matrix products  13.5 us (6%)
  local copies, waits for them, and re-layouts  12 us (6%)
  other arithmetic  3.19 us (1%)
    pallas_call x1, Pallas kernels, collect(): pl.pallas_call(collect_kernel, out_shape=(jax.ShapeDtypeStruct((tokens, f...  100 us
    pallas_call x1, Pallas kernels, dispatch(): pl.pallas_call(functools.partial(dispatch_kernel, chunk), out_shape=jax.S...  85.4 us
    unnamed x28, local copies, waits for them, and re-layouts  11 us

profile of v4, /device:TPU:0, one launch (start us, length us, event | category | flops | bytes accessed | tf_op | source)
XLA Modules:
  0.0 215.0 jit_solution(16899778875859125749)
XLA Ops:
  0.6 0.0 copy-start
  0.7 0.9 reshape.215
  1.7 0.8 convert_reduce_fusion
  2.6 0.2 select_reduce_fusion
  2.8 0.1 eq.94
  2.9 0.1 fusion.40.place_ref
  3.0 0.8 fusion.39.place_ref
  3.8 1.2 compare_convert_fusion
  5.0 2.3 %copy.16 = bf16[1024,512]{0,1:T(8,128)(2,1)} copy(bf16[1024,512]{1,0:T(8,128)(2,1)} %param.11) | data formatting | bytes 2097152 | tf_op args[2]
  7.2 0.0 copy-start.2
  7.2 1.0 copy-done.2
  8.3 0.0 copy-start.4
  8.3 1.0 copy-done.4
  9.3 0.0 copy-start.7
  9.3 0.9 copy-done.7
  10.3 0.0 copy-start.8
  10.3 1.0 copy-done.8
  11.3 85.4 %shard_map.131 = bf16[2,256,2048]{2,1,0:T(8,128)(2,1)S(1)} custom-call(bf16[128,2048]{1,0:T(8,128)(2,1)S(1)} %copy-done.8, bf16[128,2048]{1,0:T(8,128)(2,1)S(1)} %copy-done.4, bf16[512,512]{1,0:T(8,128)(2,1)S(1)} %copy-done.2, bf16[256,512]{1,0:T(8,128)(2,1)S(1)} %copy-done.7), custom_call_target="tpu_custom_call" | custom-call | tf_op jit(solution)/shard_map/pallas_call | solution.py:209
  96.7 0.0 copy-done
  96.7 0.0 copy-start.9
  96.8 1.0 fusion.2
  97.7 0.9 copy-done.9
  98.6 0.0 copy-start.10
  98.6 0.0 copy-start.11
  98.6 1.0 fusion.6
  99.6 0.9 copy-done.10
  100.5 0.0 copy-done.11
  100.5 1.2 multiply_convert_fusion.1
  101.8 2.9 %fusion.12 = bf16[1,768,2048]{2,1,0:T(8,128)(2,1)} fusion(f32[256]{0:T(256)S(1)} %bitcast.61, bf16[2,256,2048]{2,1,0:T(8,128)(2,1)S(1)} %shard_map.131, f32[256,768]{1,0:T(8,128)S(1)} %fusion.6, f32[256,768]{1,0:T(8,128)S(1)} %fusion.2), kind=kOutput, calls=%fused_computation.15 | convolution fusion | flops 809631744 | bytes 5768192 | tf_op jit(solution)/shard_map/dot_general | solution.py:519
  104.6 1.0 fusion
  105.7 0.0 copy-start.1
  105.7 0.0 copy-start.3
  105.7 0.0 copy-start.5
  105.7 0.0 copy-start.6
  105.7 1.0 fusion.16.rg_ref
  106.8 0.1 copy-done.1
  106.9 0.7 copy-done.3
  107.6 0.1 copy-done.5
  107.6 0.2 copy-done.6
  107.8 100.1 %shard_map.132 = (bf16[1024,512]{1,0:T(8,128)(2,1)S(1)}, bf16[512,512]{1,0:T(8,128)(2,1)S(1)}) custom-call(bf16[256,2048]{1,0:T(8,128)(2,1)S(1)} %fusion.16.rg_ref, bf16[512,256]{1,0:T(8,128)(2,1)S(1)} %fusion.40.place_ref, bf16[512,512]{1,0:T(8,128)(2,1)S(1)} %copy-done.6, bf16[128,2048]{1,0:T(8,128)(2,1)S(1)} %copy-done.5, bf16[512,1024]{1,0:T(8,128)(2,1)S(1)} %bitcast.57, ...), custom_call_target="tpu_custom_call" | custom-call | tf_op jit(solution)/shard_map/pallas_call | solution.py:472
  207.9 2.7 %fusion.11 = bf16[1,2048,768]{2,1,0:T(8,128)(2,1)} fusion(bf16[256,768]{1,0:T(8,128)(2,1)S(1)} %get-tuple-element.11, bf16[2,256,2048]{2,1,0:T(8,128)(2,1)S(1)} %shard_map.131), kind=kOutput, calls=%fused_computation.14 | convolution fusion | flops 806879232 | bytes 4587520 | tf_op jit(solution)/shard_map/dot_general | solution.py:525
  210.6 2.7 %fusion.10 = bf16[1,2048,768]{2,1,0:T(8,128)(2,1)} fusion(bf16[256,768]{1,0:T(8,128)(2,1)S(1)} %get-tuple-element.12, bf16[2,256,2048]{2,1,0:T(8,128)(2,1)S(1)} %shard_map.131), kind=kOutput, calls=%fused_computation.13 | convolution fusion | flops 806879232 | bytes 4587520 | tf_op jit(solution)/shard_map/dot_general | solution.py:522
  213.3 1.0 copy.20
  214.3 0.8 copy.21
  (8 shorter events, 0.1 us)
Async XLA Ops:
  0.6 96.1 %copy-start = (bf16[1,2048,768]{2,1,0:T(8,128)(2,1)S(1)}, bf16[1,2048,768]{2,1,0:T(8,128)(2,1)}, u32[]{:S(2)}) copy-start(bf16[1,2048,768]{2,1,0:T(8,128)(2,1)} %param.14) | copy-start | bytes 9437188
  7.2 1.0 copy-start.2
  8.3 1.0 copy-start.4
  9.3 0.9 copy-start.7
  10.3 1.0 copy-start.8
  96.7 1.9 copy-start.9
  98.6 1.9 copy-start.10
  98.6 1.9 copy-start.11
  105.7 1.2 copy-start.1
  105.7 1.9 copy-start.3
  105.7 2.0 copy-start.5
  105.7 2.1 copy-start.6

commit v5 on v4

--- a/solution.py
+++ b/solution.py
@@ -56,8 +56,9 @@
 
 
 def dispatch_kernel(
-    chunk, in_ref, grad_ref, pick_ref, place_ref, out_ref, gat, stage, recv,
-    up_s, up_r, down_s, down_r, plane_s, plane_r, own_s,
+    chunk, in_ref, grad_ref, gate_hbm, up_hbm, down_hbm, pick_ref, place_ref, scale_ref,
+    rows_ref, scaled_ref, gate_ref, upper_ref, back_ref, gat, stage, recv, gate_w, up_w, down_w,
+    up_s, up_r, down_s, down_r, plane_s, plane_r, own_s, w_s,
 ):
     groups, nz, ny, g, z, y = place()
     planes = groups * ny
@@ -76,8 +77,14 @@
         taken = ref.at[:, pl.ds((i % parts) * chunk, chunk)]
         return pltpu.make_async_copy(taken, gat.at[i, here], own_s.at[i])
 
+    weights = [
+        pltpu.make_async_copy(src, dst, w_s.at[n])
+        for n, (src, dst) in enumerate([(gate_hbm, gate_w), (up_hbm, up_w), (down_hbm, down_w)])
+    ]
     for i in range(items):
         fetch(i).start()
+    for copy in weights:
+        copy.start()
     greet(g, z, y, nz, ny, planes)
 
     def cols(i):
@@ -151,10 +158,34 @@
             return carry
 
         lax.fori_loop(1, planes, one, 0)
-        out_ref[a, :, cols(i)] = jnp.dot(
+        rows = jnp.dot(
             place_ref[...], recv[i], preferred_element_type=jnp.float32
         ).astype(jnp.bfloat16)
 
+        @pl.when(i == 0)
+        def _():
+            weights[0].wait()
+            weights[1].wait()
+            weights[2].wait()
+
+        @pl.when(a == 0)
+        def _():
+            rows_ref[:, cols(i)] = rows
+            gate_ref[...] += jnp.dot(rows, gate_w[cols(i), :], preferred_element_type=jnp.float32)
+            upper_ref[...] += jnp.dot(rows, up_w[cols(i), :], preferred_element_type=jnp.float32)
+
+        @pl.when(a == 1)
+        def _():
+            scaled = (rows.astype(jnp.float32) * scale_ref[...]).astype(jnp.bfloat16)
+            scaled_ref[:, cols(i)] = scaled
+            back_ref[...] += lax.dot_general(
+                scaled, down_w[:, cols(i)], (((1,), (1,)), ((), ())),
+                preferred_element_type=jnp.float32,
+            )
+
+    gate_ref[...] = jnp.zeros_like(gate_ref)
+    upper_ref[...] = jnp.zeros_like(upper_ref)
+    back_ref[...] = jnp.zeros_like(back_ref)
     for i in range(items):
         fetch(i).wait()
 
@@ -198,8 +229,9 @@
     lax.fori_loop(0, items, drain, 0)
 
 
-def dispatch(moe_input, out_grad, picker, placer, nz, planes):
+def dispatch(moe_input, out_grad, gate_w, up_w, down_w, picker, placer, scales, nz, planes):
     rows, width = moe_input.shape
+    hidden = gate_w.shape[1]
     taken = placer.shape[1]
     cap = placer.shape[0]
     chunk = width // 4
@@ -208,27 +240,31 @@
     vmem = pl.BlockSpec(memory_space=pltpu.VMEM)
     return pl.pallas_call(
         functools.partial(dispatch_kernel, chunk),
-        out_shape=jax.ShapeDtypeStruct((2, cap, width), jnp.bfloat16),
-        in_specs=[pl.BlockSpec(memory_space=pl.ANY)] * 2 + [vmem] * 2,
-        out_specs=vmem,
+        out_shape=[jax.ShapeDtypeStruct((cap, width), jnp.bfloat16)] * 2
+        + [jax.ShapeDtypeStruct((cap, hidden), jnp.float32)] * 3,
+        in_specs=[pl.BlockSpec(memory_space=pl.ANY)] * 5 + [vmem] * 3,
+        out_specs=[vmem] * 5,
         scratch_shapes=[
             pltpu.VMEM((items, nz * rows, chunk), jnp.bfloat16),
             pltpu.VMEM((items, taken, chunk), jnp.bfloat16),
             pltpu.VMEM((items, taken, chunk), jnp.bfloat16),
+            pltpu.VMEM(gate_w.shape, jnp.bfloat16),
+            pltpu.VMEM(up_w.shape, jnp.bfloat16),
+            pltpu.VMEM(down_w.shape, jnp.bfloat16),
             dma((items, nz - 1)), dma((items, nz - 1)),
             dma((items, nz - 1)), dma((items, nz - 1)),
             dma((items, planes - 1)), dma((items, planes - 1)),
-            dma((items,)),
+            dma((items,)), dma((3,)),
         ],
         compiler_params=pltpu.CompilerParams(
-            collective_id=0, has_side_effects=True, vmem_limit_bytes=24 * 2**20
+            collective_id=0, has_side_effects=True, vmem_limit_bytes=48 * 2**20
         ),
-    )(moe_input, out_grad, picker, placer)
+    )(moe_input, out_grad, gate_w, up_w, down_w, picker, placer, scales)
 
 
 def collect_kernel(
     rg_ref, place_ref, pick_ref, og_ref, context_ref, wout_ref, ctx_ref, proj_ref,
-    stage, recv, part, piece, ctx, proj, proj_in, to_line, from_line,
+    stage, recv, part, piece, ctx, proj, proj_in, to_line, from_line, context_t,
     plane_s, plane_r, sum_s, sum_r, up_s, up_r, down_s, down_r, y_s, y_r, proj_s, proj_r,
 ):
     groups, nz, ny, g, z, y = place()
@@ -389,7 +425,7 @@
             ctx[...] += term
 
         share_of = lax.dot_general(
-            context_ref[...], totals, (((1,), (0,)), ((), ())),
+            context_t[...], totals, (((1,), (0,)), ((), ())),
             preferred_element_type=jnp.float32,
         )
 
@@ -424,6 +460,10 @@
             @pl.when((t >= k) & (t - k < parts))
             def _():
                 stages[k](t - k)
+
+        @pl.when(t == 0)
+        def _():
+            context_t[...] = context_ref[...].T
 
         return carry
 
@@ -487,6 +527,7 @@
             pltpu.VMEM((parts - 1, features, chunk), jnp.bfloat16),
             pltpu.VMEM(line, jnp.bfloat16),
             pltpu.VMEM(line, jnp.bfloat16),
+            pltpu.VMEM((features, tokens), jnp.bfloat16),
             dma((parts, planes - 1)), dma((parts, planes - 1)),
             dma((parts, nz - 1)), dma((parts, nz - 1)),
             dma((parts, nz - 1)), dma((parts, nz - 1)),
@@ -495,21 +536,17 @@
             dma((parts - 1,)), dma((parts - 1,)),
         ],
         compiler_params=pltpu.CompilerParams(
-            collective_id=1, has_side_effects=True, vmem_limit_bytes=40 * 2**20
+            collective_id=1, has_side_effects=True, vmem_limit_bytes=44 * 2**20
         ),
     )(row_grad, placer, picker, out_grad, context, w_out)
 
 
-def expert_backward(rows_in, rows_grad, scales, gate_w, up_w, down_w):
-    gate_pre = jnp.dot(rows_in, gate_w, preferred_element_type=jnp.float32)
-    up_pre = jnp.dot(rows_in, up_w, preferred_element_type=jnp.float32)
+def expert_backward(rows_in, scaled, gate_pre, up_pre, back_hidden, gate_w, up_w):
     sig = jax.nn.sigmoid(gate_pre)
     silu = gate_pre * sig
     hidden = (silu * up_pre).astype(jnp.bfloat16)
-    scaled = (rows_grad.astype(jnp.float32) * scales[:, None]).astype(jnp.bfloat16)
     outer = (((0,), (0,)), ((), ()))
     inner_dims = (((1,), (1,)), ((), ()))
-    back_hidden = lax.dot_general(scaled, down_w, inner_dims, preferred_element_type=jnp.float32)
     back_gate = (back_hidden * up_pre * sig * (1.0 + gate_pre * (1.0 - sig))).astype(jnp.bfloat16)
     back_up = (back_hidden * silu).astype(jnp.bfloat16)
     row_grad = lax.dot_general(back_gate, gate_w, inner_dims, preferred_element_type=jnp.float32)
@@ -569,12 +606,15 @@
     capacity = selected.shape[1]
     most = max(4, (2 * capacity + devices - 1) // devices)
     picker, placer = tables(selected, tok_rows, most)
-    rows = dispatch(moe_input, out_grad, picker, placer, nz, planes)
+    rows_in, scaled, gate_pre, up_pre, back_hidden = dispatch(
+        moe_input, out_grad, w_gate[0], w_up[0], w_down[0], picker, placer,
+        gate_scale[0][:, None], nz, planes,
+    )
     grad_gate, grad_up, grad_down, row_grad = expert_backward(
-        rows[0], rows[1], gate_scale[0], w_gate[0], w_up[0], w_down[0]
+        rows_in, scaled, gate_pre, up_pre, back_hidden, w_gate[0], w_up[0]
     )
     grad_ctx, grad_proj = collect(
-        row_grad, placer.T, picker.T, out_grad, context.T, w_out, groups, nz, ny
+        row_grad, placer.T, picker.T, out_grad, context, w_out, groups, nz, ny
     )
     return (
         grad_gate[None],

time: 218 us -> 211 us (0.968)
  local copies, waits for them, and re-layouts: 12 us -> 8.14 us
  matrix products: 13.5 us -> 10.2 us
    unnamed x28 -> x19, local copies, waits for them, and re-layouts: 11 us -> 6.47 us
    dot_general x3 -> x0, matrix products: 3.2 us -> none  [the longest x1 1.24 us: expert_backward(): lax.dot_general(scaled, down_w, inner_dims, preferred_element_type=jnp.fl...]
where the time goes in v5:
time: 211 us; the launch traced here: 208 us
  Pallas kernels  187 us (89%)
  matrix products  10.2 us (5%)
  local copies, waits for them, and re-layouts  8.14 us (4%)
    pallas_call x1, Pallas kernels, collect(): pl.pallas_call(collect_kernel, out_shape=(jax.ShapeDtypeStruct((tokens, f...  100 us
    pallas_call x1, Pallas kernels, dispatch(): pl.pallas_call(functools.partial(dispatch_kernel, chunk), out_shape=[jax....  86.9 us
    unnamed x19, local copies, waits for them, and re-layouts  6.47 us

profile of v5, /device:TPU:0, one launch (start us, length us, event | category | flops | bytes accessed | tf_op | source)
XLA Modules:
  0.0 208.1 jit_solution(18083587067000328375)
XLA Ops:
  0.7 0.8 reshape.205
  1.6 0.8 convert_reduce_fusion
  2.4 0.2 select_reduce_fusion
  2.6 0.1 eq.94
  2.7 0.8 copy.16.scale_ref
  3.5 0.1 fusion.7.place_ref
  3.6 0.1 fusion.6.place_ref
  3.7 0.2 compare_convert_fusion
  4.0 0.0 copy-start.1
  4.0 1.0 copy-done.1
  5.0 0.0 copy-start.4
  5.0 1.0 copy-done.4
  6.1 86.9 %shard_map.128 = (bf16[256,2048]{1,0:T(8,128)(2,1)S(1)}, bf16[256,2048]{1,0:T(8,128)(2,1)}, f32[256,768]{1,0:T(8,128)S(1)}, f32[256,768]{1,0:T(8,128)S(1)}, f32[256,768]{1,0:T(8,128)S(1)}) custom-call(bf16[128,2048]{1,0:T(8,128)(2,1)S(1)} %copy-done.4, bf16[128,2048]{1,0:T(8,128)(2,1)S(1)} %copy-done.1, bf16[2048,768]{1,0:T(8,128)(2,1)} %bitcast.27, ...), custom_call_target="tpu_custom_call" | custom-call | tf_op jit(solution)/shard_map/pallas_call | solution.py:241
  93.0 0.0 copy-start.7
  93.0 0.4 multiply_convert_fusion.1
  93.4 0.8 copy-done.7
  94.2 0.0 copy-start.6
  94.2 2.7 %fusion.2 = bf16[1,768,2048]{2,1,0:T(8,128)(2,1)} fusion(bf16[256,2048]{1,0:T(8,128)(2,1)S(1)} %copy-done.7, f32[256,768]{1,0:T(8,128)S(1)} %get-tuple-element.14, f32[256,768]{1,0:T(8,128)S(1)} %get-tuple-element.15), kind=kOutput, calls=%fused_computation.5 | convolution fusion | flops 808058880 | bytes 5767168 | tf_op jit(solution)/shard_map/dot_general | solution.py:556
  97.0 0.0 copy-done.6
  97.0 0.0 copy-start.5
  97.0 1.0 fusion.21
  98.0 0.9 copy-done.5
  98.9 0.0 copy-start
  98.9 0.0 copy-start.2
  98.9 0.0 copy-start.3
  98.9 1.0 fusion.3.rg_ref
  99.9 0.5 copy-done
  100.5 0.1 copy-done.2
  100.5 0.3 copy-done.3
  100.9 100.1 %shard_map.129 = (bf16[1024,512]{1,0:T(8,128)(2,1)S(1)}, bf16[512,512]{1,0:T(8,128)(2,1)S(1)}) custom-call(bf16[256,2048]{1,0:T(8,128)(2,1)S(1)} %fusion.3.rg_ref, bf16[512,256]{1,0:T(8,128)(2,1)S(1)} %fusion.7.place_ref, bf16[512,512]{1,0:T(8,128)(2,1)S(1)} %get-tuple-element.25.pick_ref, bf16[128,2048]{1,0:T(8,128)(2,1)S(1)} %copy-done.2, ...), custom_call_target="tpu_custom_call" | custom-call | tf_op jit(solution)/shard_map/pallas_call | solution.py:512
  200.9 2.7 %fusion.1 = bf16[1,2048,768]{2,1,0:T(8,128)(2,1)} fusion(bf16[256,2048]{1,0:T(8,128)(2,1)S(1)} %get-tuple-element.12, bf16[256,768]{1,0:T(8,128)(2,1)S(1)} %get-tuple-element.21), kind=kOutput, calls=%fused_computation.4 | convolution fusion | flops 806879232 | bytes 4587520 | tf_op jit(solution)/shard_map/dot_general | solution.py:562
  203.6 2.7 %fusion = bf16[1,2048,768]{2,1,0:T(8,128)(2,1)} fusion(bf16[256,2048]{1,0:T(8,128)(2,1)S(1)} %get-tuple-element.12, bf16[256,768]{1,0:T(8,128)(2,1)S(1)} %get-tuple-element.22), kind=kOutput, calls=%fused_computation.3 | convolution fusion | flops 806879232 | bytes 4587520 | tf_op jit(solution)/shard_map/dot_general | solution.py:559
  206.3 1.0 copy.20
  207.3 0.8 copy.21
  (8 shorter events, 0.1 us)
Async XLA Ops:
  4.0 1.0 copy-start.1
  5.0 1.0 copy-start.4
  93.0 1.2 copy-start.7
  94.2 2.8 %copy-start.6 = (bf16[1,2048,768]{2,1,0:T(8,128)(2,1)S(1)}, bf16[1,2048,768]{2,1,0:T(8,128)(2,1)}, u32[]{:S(2)}) copy-start(bf16[1,2048,768]{2,1,0:T(8,128)(2,1)} %param.14) | copy-start | bytes 9437188
  97.0 1.9 copy-start.5
  98.9 1.6 copy-start
  98.9 1.7 copy-start.2
  98.9 2.0 copy-start.3

commit v6 on v5

--- a/solution.py
+++ b/solution.py
@@ -257,7 +257,7 @@
             dma((items,)), dma((3,)),
         ],
         compiler_params=pltpu.CompilerParams(
-            collective_id=0, has_side_effects=True, vmem_limit_bytes=48 * 2**20
+            collective_id=0, has_side_effects=True, vmem_limit_bytes=58 * 2**20
         ),
     )(moe_input, out_grad, gate_w, up_w, down_w, picker, placer, scales)
 
@@ -449,11 +449,17 @@
             (owner(q, g), z * ny + y),
         )
 
-    stages = [scatter, gathered, total]
+    stages = [gathered, total]
     stages += [functools.partial(lambda s, q: forward(q, s), s) for s in range(1, nz)]
     stages += [project]
 
     last = len(stages) - 1
+
+    def begin(q, carry):
+        scatter(q)
+        return carry
+
+    lax.fori_loop(0, parts, begin, 0)
 
     def step(t, carry):
         for k in [*reversed(range(last)), last]:

time: 211 us -> 216 us (1.024)
  Pallas kernels: 187 us -> 191 us
  other arithmetic: 1.95 us -> 5.14 us
    pallas_call x1, Pallas kernels: 86.9 us -> 89.7 us  [dispatch(): pl.pallas_call(functools.partial(dispatch_kernel, chunk), out_shape=[jax....]
    unnamed x19 -> x21, local copies, waits for them, and re-layouts: 6.47 us -> 3.88 us
where the time goes in v6:
time: 216 us; the launch traced here: 214 us
  Pallas kernels  191 us (88%)
  matrix products  10.2 us (5%)
  local copies, waits for them, and re-layouts  6.23 us (3%)
  other arithmetic  5.14 us (2%)
    pallas_call x1, Pallas kernels, collect(): pl.pallas_call(collect_kernel, out_shape=(jax.ShapeDtypeStruct((tokens, f...  102 us
    pallas_call x1, Pallas kernels, dispatch(): pl.pallas_call(functools.partial(dispatch_kernel, chunk), out_shape=[jax....  89.7 us

profile of v6, /device:TPU:0, one launch (start us, length us, event | category | flops | bytes accessed | tf_op | source)
XLA Modules:
  0.0 213.8 jit_solution(12217306649759722459)
XLA Ops:
  0.7 0.8 reshape.205
  1.6 0.8 convert_reduce_fusion
  2.4 0.2 select_reduce_fusion
  2.6 0.1 eq.94
  2.7 1.5 copy.16.scale_ref
  4.2 0.1 fusion.7.place_ref
  4.3 0.8 fusion.6.place_ref
  5.1 1.0 compare_convert_fusion
  6.1 89.7 %shard_map.128 = (bf16[256,2048]{1,0:T(8,128)(2,1)}, bf16[256,2048]{1,0:T(8,128)(2,1)}, f32[256,768]{1,0:T(8,128)}, f32[256,768]{1,0:T(8,128)}, f32[256,768]{1,0:T(8,128)}) custom-call(bf16[128,2048]{1,0:T(8,128)(2,1)} %in_ref.1, bf16[128,2048]{1,0:T(8,128)(2,1)} %og_ref.1, bf16[2048,768]{1,0:T(8,128)(2,1)} %bitcast.27, bf16[2048,768]{1,0:T(8,128)(2,1)} %bitcast.26, ...), custom_call_target="tpu_custom_call" | custom-call | tf_op jit(solution)/shard_map/pallas_call | solution.py:241
  95.8 0.0 copy-start.5
  95.8 0.0 copy-start.6
  95.8 0.0 copy-start.8
  95.8 2.1 %multiply_convert_fusion.1 = (bf16[256,768]{1,0:T(8,128)(2,1)S(1)}, bf16[256,768]{1,0:T(8,128)(2,1)S(1)}) fusion(f32[256,768]{1,0:T(8,128)} %get-tuple-element.13, f32[256,768]{1,0:T(8,128)} %get-tuple-element.15, f32[256,768]{1,0:T(8,128)} %get-tuple-element.14), kind=kLoop, calls=%fused_computation.12 | loop fusion | flops 2555904 | bytes 3145728 | tf_op jit(solution)/shard_map/convert_element_type | solution.py:557
  98.0 0.0 copy-done.5
  98.0 0.0 copy-done.6
  98.0 0.2 copy-done.8
  98.2 0.0 copy-start.4
  98.2 2.7 %fusion.2 = bf16[1,768,2048]{2,1,0:T(8,128)(2,1)} fusion(bf16[256,2048]{1,0:T(8,128)(2,1)S(1)} %copy-done.8, f32[256,768]{1,0:T(8,128)S(1)} %copy-done.6, f32[256,768]{1,0:T(8,128)S(1)} %copy-done.5), kind=kOutput, calls=%fused_computation.5 | convolution fusion | flops 808058880 | bytes 5767168 | tf_op jit(solution)/shard_map/dot_general | solution.py:562
  100.9 0.0 copy-done.4
  100.9 0.0 copy-start.3
  100.9 1.0 fusion.21
  102.0 0.9 copy-done.3
  102.8 0.0 copy-start
  102.8 0.0 copy-start.1
  102.8 0.0 copy-start.2
  102.8 1.0 fusion.3.rg_ref
  103.9 0.6 copy-done
  104.4 0.1 copy-done.1
  104.5 0.3 copy-done.2
  104.8 0.0 copy-start.7
  104.8 101.7 %shard_map.129 = (bf16[1024,512]{1,0:T(8,128)(2,1)S(1)}, bf16[512,512]{1,0:T(8,128)(2,1)S(1)}) custom-call(bf16[256,2048]{1,0:T(8,128)(2,1)S(1)} %fusion.3.rg_ref, bf16[512,256]{1,0:T(8,128)(2,1)S(1)} %fusion.7.place_ref, bf16[512,512]{1,0:T(8,128)(2,1)S(1)} %get-tuple-element.25.pick_ref, bf16[128,2048]{1,0:T(8,128)(2,1)S(1)} %copy-done.1, ...), custom_call_target="tpu_custom_call" | custom-call | tf_op jit(solution)/shard_map/pallas_call | solution.py:518
  206.6 0.0 copy-done.7
  206.6 2.7 %fusion.1 = bf16[1,2048,768]{2,1,0:T(8,128)(2,1)} fusion(bf16[256,2048]{1,0:T(8,128)(2,1)S(1)} %copy-done.7, bf16[256,768]{1,0:T(8,128)(2,1)S(1)} %get-tuple-element.21), kind=kOutput, calls=%fused_computation.4 | convolution fusion | flops 806879232 | bytes 4587520 | tf_op jit(solution)/shard_map/dot_general | solution.py:568
  209.3 2.7 %fusion = bf16[1,2048,768]{2,1,0:T(8,128)(2,1)} fusion(bf16[256,2048]{1,0:T(8,128)(2,1)S(1)} %copy-done.7, bf16[256,768]{1,0:T(8,128)(2,1)S(1)} %get-tuple-element.22), kind=kOutput, calls=%fused_computation.3 | convolution fusion | flops 806879232 | bytes 4587520 | tf_op jit(solution)/shard_map/dot_general | solution.py:565
  212.0 1.0 copy.20
  213.0 0.8 copy.21
  (8 shorter events, 0.1 us)
Async XLA Ops:
  95.8 2.2 %copy-start.5 = (f32[256,768]{1,0:T(8,128)S(1)}, f32[256,768]{1,0:T(8,128)}, u32[]{:S(2)}) copy-start(f32[256,768]{1,0:T(8,128)} %get-tuple-element.15) | copy-start | bytes 2359300
  95.8 2.2 %copy-start.6 = (f32[256,768]{1,0:T(8,128)S(1)}, f32[256,768]{1,0:T(8,128)}, u32[]{:S(2)}) copy-start(f32[256,768]{1,0:T(8,128)} %get-tuple-element.14) | copy-start | bytes 2359300
  95.8 2.4 %copy-start.8 = (bf16[256,2048]{1,0:T(8,128)(2,1)S(1)}, bf16[256,2048]{1,0:T(8,128)(2,1)}, u32[]{:S(2)}) copy-start(bf16[256,2048]{1,0:T(8,128)(2,1)} %get-tuple-element.16) | copy-start | bytes 3145732
  98.2 2.7 %copy-start.4 = (bf16[1,2048,768]{2,1,0:T(8,128)(2,1)S(1)}, bf16[1,2048,768]{2,1,0:T(8,128)(2,1)}, u32[]{:S(2)}) copy-start(bf16[1,2048,768]{2,1,0:T(8,128)(2,1)} %param.14) | copy-start | bytes 9437188
  100.9 1.9 copy-start.3
  102.8 1.6 copy-start
  102.8 1.7 copy-start.1
  102.8 2.0 copy-start.2
  104.8 101.7 %copy-start.7 = (bf16[256,2048]{1,0:T(8,128)(2,1)S(1)}, bf16[256,2048]{1,0:T(8,128)(2,1)}, u32[]{:S(2)}) copy-start(bf16[256,2048]{1,0:T(8,128)(2,1)} %get-tuple-element.12) | copy-start | bytes 3145732
